TPU v7x, 256 devices: a whole 4x4x8 slice. The times are simulated.
256 devices in a mesh: dp: 16 (over z_lo, y, core), fsdp: 16 (over x, z_hi).
Axes of the slice: x: 4, y: 4, z: 8 (z_hi: 4, z_lo: 2; z = z_hi * 2 + z_lo), core: 2. Of those that a mesh axis runs over, the one named last changes fastest.
Arguments:
- rows_owned: bfloat16 [16, 16, 256, 8192], P('dp', 'fsdp'), may hold values from -6 to 6
- target: int32 [16, 16, 256], P('dp', 'fsdp'), may hold values from 0 to 15, as said below
- offset: int32 [16, 16, 256], P('dp', 'fsdp'), may hold values from 0 to 255, as said below
- queries: bfloat16 [16, 16, 256, 4096], P('dp', 'fsdp'), may hold values from -6 to 6
- keys: bfloat16 [16, 16, 256, 512], P('dp', 'fsdp'), may hold values from -6 to 6
- cotangent: bfloat16 [16, 16, 256, 4096], P('dp', 'fsdp'), may hold values from -0.0234375 to 0.0234375
- segment: int32 [16, 16, 256], P('dp', 'fsdp'), may hold values from 0 to 15, as said below
- norm_gain: bfloat16 [8192], P('fsdp'), may hold values from 0.099609375 to 1.8984375
- value_weight: bfloat16 [8192, 512], P('fsdp'), may hold values from -0.0625 to 0.0625
Outputs:
- returned: bfloat16 [16, 16, 256, 4096], P('dp', 'fsdp')
- value_grad_sum: float32 [8192, 512], P('fsdp')
Inputs may be any that keep to these rules, and one draw needn't show every extreme that they name: `target`: within one fsdp index, every owner device sends exactly one rollout, a run of consecutive rows, to every trainer device of its dp group, the rollouts in order of trainer index; at most 32 rows go from one owner device to one trainer device, and exactly 32 for some pair. Within one fsdp index the pairs (target, offset) of all owner rows are distinct, so that every packed row of every trainer device receives exactly one row; consecutive rows of a rollout keep consecutive offsets. `segment`: equal ids on a trainer device mark the rows of one rollout, which stand together; ids never fall along a device's rows; the id of a packed row is the dp index of the owner device that sent it.
All inputs are finite; a program needn't handle non-finite values.
Results may differ from a plain program's by a relative error of at most 0.025.
Values may be sent and summed in bfloat16 or wider, within the bound.
A program may use at most 128 MiB of HBM per device.

v0:
```python
import math

import jax
import jax.numpy as jnp
from jax import lax
from jax.sharding import PartitionSpec as P

HEAD_DIM = 128
HEADS_Q = 32
KV_HEADS = 4


epsilon = 1e-05


def normalize(rows, gain_full):
    widened = rows.astype(jnp.float32)
    inverse = lax.rsqrt(jnp.mean(widened * widened, axis=1, keepdims=True) + epsilon)
    return (widened * inverse * gain_full.astype(jnp.float32)[None, :]).astype(jnp.bfloat16)


def project(normed, weight_full):
    return jnp.dot(normed, weight_full, preferred_element_type=jnp.float32).astype(jnp.bfloat16)


def softmax_weights(queries, keys, segment):
    row_count = queries.shape[0]
    group_size = HEADS_Q // KV_HEADS
    query_heads = queries.reshape(row_count, KV_HEADS, group_size, HEAD_DIM)
    key_heads = keys.reshape(row_count, KV_HEADS, HEAD_DIM)
    scores = jnp.einsum(
        "qgsd,kgd->gsqk", query_heads, key_heads, preferred_element_type=jnp.float32
    ) * (1.0 / math.sqrt(HEAD_DIM))
    position = jnp.arange(row_count, dtype=jnp.int32)
    allowed = (segment[:, None] == segment[None, :]) & (position[None, :] <= position[:, None])
    scores = jnp.where(allowed[None, None], scores, -1e30)
    highest = jnp.max(scores, axis=-1, keepdims=True)
    powers = jnp.exp(scores - highest)
    return (powers / jnp.sum(powers, axis=-1, keepdims=True)).astype(jnp.bfloat16)


def gather_weights(norm_gain, value_weight):
    gain_full, weight_full = (
        lax.all_gather(norm_gain, "fsdp", axis=0, tiled=True),
        lax.all_gather(value_weight, "fsdp", axis=0, tiled=True),
    )
    return (gain_full, weight_full)


def on_device(
    rows_owned, target, offset, queries, keys, cotangent, segment, norm_gain, value_weight
):
    row_count = rows_owned.shape[2]
    feature_width = rows_owned.shape[3]
    owned = rows_owned.reshape(row_count, feature_width)
    targets = target.reshape(row_count)
    positions = offset.reshape(row_count)
    peer_count = lax.axis_size("dp")
    capacity = 2 * row_count // peer_count
    chosen = (targets[:, None] == jnp.arange(peer_count, dtype=jnp.int32)[None, :]).astype(
        jnp.int32
    )
    earlier = jnp.cumsum(chosen, axis=0) - chosen
    slot_index = jnp.sum(earlier * chosen, axis=1)
    send_positions = (
        jnp.full((peer_count, capacity), row_count, jnp.int32)
        .at[targets, slot_index]
        .set(positions)
    )
    gain_full, weight_full = gather_weights(norm_gain, value_weight)
    value_width = weight_full.shape[1]
    normed_own = normalize(owned, gain_full)
    send_rows = (
        jnp.zeros((peer_count, capacity, feature_width), owned.dtype)
        .at[targets, slot_index]
        .set(owned)
    )
    got_rows, got_positions = (
        lax.all_to_all(send_rows, "dp", split_axis=0, concat_axis=0, tiled=True),
        lax.all_to_all(send_positions, "dp", split_axis=0, concat_axis=0, tiled=True),
    )
    landing = got_positions.reshape(peer_count * capacity)
    packed = (
        jnp.zeros((row_count, feature_width), owned.dtype)
        .at[landing]
        .set(got_rows.reshape(peer_count * capacity, feature_width), mode="drop")
    )
    values = project(normalize(packed, gain_full), weight_full)
    query_rows = queries.reshape(row_count, HEADS_Q * HEAD_DIM)
    key_rows = keys.reshape(row_count, KV_HEADS * HEAD_DIM)
    probabilities = softmax_weights(query_rows, key_rows, segment.reshape(row_count))
    group_size = HEADS_Q // KV_HEADS
    value_heads = values.reshape(row_count, KV_HEADS, HEAD_DIM)
    attended = jnp.einsum(
        "gsqk,kgd->qgsd", probabilities, value_heads, preferred_element_type=jnp.float32
    )
    attended = attended.astype(jnp.bfloat16).reshape(row_count, HEADS_Q * HEAD_DIM)
    upstream = cotangent.reshape(row_count, KV_HEADS, group_size, HEAD_DIM)
    packed_grad = jnp.einsum(
        "gsqk,qgsd->kgd", probabilities, upstream, preferred_element_type=jnp.float32
    )
    packed_grad = packed_grad.astype(jnp.bfloat16).reshape(row_count, value_width)
    gather_rows = jnp.minimum(landing, row_count - 1)
    outgoing = attended[gather_rows].reshape(peer_count, capacity, HEADS_Q * HEAD_DIM)
    outgoing_grad = packed_grad[gather_rows].reshape(peer_count, capacity, value_width)
    returned, returned_grad = (
        lax.all_to_all(outgoing, "dp", split_axis=0, concat_axis=0, tiled=True),
        lax.all_to_all(outgoing_grad, "dp", split_axis=0, concat_axis=0, tiled=True),
    )
    own_rows = returned[targets, slot_index].reshape(1, 1, row_count, HEADS_Q * HEAD_DIM)
    owner_grad = returned_grad[targets, slot_index]
    shard_sum = lax.psum_scatter(
        lax.dot_general(
            normed_own, owner_grad, (((0,), (0,)), ((), ())), preferred_element_type=jnp.float32
        ).astype(jnp.bfloat16),
        "fsdp",
        scatter_dimension=0,
        tiled=True,
    )
    gradient = lax.psum(shard_sum, "dp").astype(jnp.float32)
    return (own_rows, gradient)


def solution(mesh):
    placed = (
        P("dp", "fsdp", None, None),
        P("dp", "fsdp", None),
        P("dp", "fsdp", None),
        P("dp", "fsdp", None, None),
        P("dp", "fsdp", None, None),
        P("dp", "fsdp", None, None),
        P("dp", "fsdp", None),
        P("fsdp"),
        P("fsdp", None),
    )
    return jax.shard_map(
        on_device,
        mesh=mesh,
        in_specs=placed,
        out_specs=(P("dp", "fsdp", None, None), P("fsdp", None)),
        check_vma=False,
    )
```

profile of v0, /device:TPU:1, one launch (start us, length us, event | category | flops | bytes accessed | tf_op | source)
XLA Modules:
  0.0 677.8 jit_solution(9137113583349018280)
XLA Ops:
  7.2 0.0 all-gather.3.cloned.1.call-start
  7.2 0.7 all-gather.3.cloned.1.call-update
  7.9 0.7 fusion.31
  8.6 0.6 reduce-window.6
  9.2 0.2 slice_reduce_fusion
  9.4 0.8 fusion.30
  10.2 0.7 or_select_fusion
  10.9 0.6 broadcast_in_dim.15
  11.5 39.0 %scatter_fusion = s32[16,32]{1,0:T(8,128)} fusion(s32[16,32]{1,0:T(8,128)} %broadcast_in_dim.15, s32[256]{0:T(256)S(1)} %bitcast.93, s32[256]{0:T(256)} %bitcast.113), kind=kCustom, calls=%fused_computation.4 | custom fusion | bytes 5120 | tf_op jit(solution)/shard_map/scatter | solution.py:68
  50.5 7.4 %all-to-all-start = ((s32[16,1,32]{2,1,0:T(1,128)}), s32[16,1,32]{2,1,0:T(1,128)S(1)}, u32[]{:S(2)}, u32[]{:S(2)}) async-start(s32[16,1,32]{2,1,0:T(1,128)} %bitcast.8), calls=%async_computation | async-start | bytes 16384 | tf_op jit(solution)/shard_map/all_to_all | solution.py:80
  57.9 2.5 copy.48
  60.4 0.1 reshape_reshape.6
  60.4 4.1 copy.46
  64.5 0.1 fusion.27
  64.6 1.4 fusion.18
  66.0 2.4 fusion.37
  68.4 1.1 divide_convert_fusion
  69.5 0.5 copy-done.1
  70.0 1.5 fusion.25
  71.5 0.0 copy-done
  71.5 0.1 copy.37
  71.7 0.5 broadcast.263
  72.2 0.7 reduce.5
  72.9 0.1 reshape.216
  73.0 2.6 gather_fusion.2
  75.6 5.6 all-to-all-start.3
  81.2 4.2 broadcast_in_dim.16
  85.4 128.7 %scatter_fusion.1 = bf16[16,32,8192]{2,1,0:T(8,128)(2,1)} fusion(bf16[16,32,8192]{2,1,0:T(8,128)(2,1)} %broadcast_in_dim.16, s32[256]{0:T(256)S(1)} %bitcast.94, bf16[256,8192]{1,0:T(8,128)(2,1)} %bitcast.95), kind=kCustom, calls=%fused_computation.5 | custom fusion | bytes 12584960 | tf_op jit(solution)/shard_map/scatter | solution.py:76
  214.1 7.4 %all-to-all-start.1 = ((bf16[16,32,8192]{2,1,0:T(8,128)(2,1)}), bf16[16,32,8192]{2,1,0:T(8,128)(2,1)}, u32[]{:S(2)}, u32[]{:S(2)}) async-start(bf16[16,32,8192]{2,1,0:T(8,128)(2,1)} %scatter_fusion.1), calls=%async_computation.1 | async-start | bytes 16777216 | tf_op jit(solution)/shard_map/all_to_all | solution.py:79
  221.5 0.0 reduce-scatter.2.cloned.1.call-start
  221.6 153.5 %all-gather = bf16[16,1,512]{2,1,0:T(2,128)(2,1)S(1)} all-gather(bf16[1,1,512]{2,1,0:T(2,128)(2,1)S(1)} %reshape.274), channel_id=1, replica_groups=mesh['dp'=16,'fsdp'=16] {'fsdp'}, dimensions={0}, use_global_device_ids=true | all-gather | bytes 17408 | tf_op jit(solution)/shard_map/all_gather | solution.py:44
  375.1 3.1 fusion.4
  378.2 2.1 gather_fusion.3
  380.3 8.2 %convolution_convert_fusion = bf16[8192,512]{1,0:T(8,128)(2,1)} fusion(bf16[256,512]{1,0:T(8,128)(2,1)S(1)} %gather_fusion.3, f32[256]{0:T(256)S(1)} %add_rsqrt_fusion, f32[8192]{0:T(1024)S(1)} %bitcast.105, bf16[1,1,256,8192]{3,2,1,0:T(8,128)(2,1)} %param.9), kind=kOutput, calls=%fused_computation.8 | convolution fusion | flops 2160066560 | bytes 12878848 | tf_op jit(solution)/shard_map/dot_general | solution.py:113
  388.5 16.7 %scatter_custom_fusion.2 = bf16[256,8192]{1,0:T(8,128)(2,1)} fusion(s32[512]{0:T(512)S(1)} %bitcast.112, bf16[512,8192]{1,0:T(8,128)(2,1)} %bitcast.11, bf16[]{:T(256)} %constant.12.clone.1), kind=kCustom, calls=%fused_computation.33 | custom fusion | bytes 4194816 | tf_op jit(solution)/shard_map/scatter | solution.py:86
  405.2 3.1 fusion.1
  408.3 0.0 all-gather.3.cloned.1.call-done
  408.4 7.1 %fusion.22 = bf16[256,512]{1,0:T(8,128)(2,1)S(1)} fusion(bf16[8192,512]{1,0:T(8,128)(2,1)} %all-gather.3.cloned.1.call-done, bf16[256,8192]{1,0:T(8,128)(2,1)} %scatter_custom_fusion.2, f32[8192]{0:T(1024)S(1)} %bitcast.106, f32[256]{0:T(256)S(1)} %add_rsqrt_fusion.1), kind=kOutput, calls=%fused_computation.37 | convolution fusion | flops 2156003328 | bytes 12878848 | tf_op jit(solution)/shard_map/dot_general | solution.py:23
  415.5 0.1 copy.43
  415.6 4.3 convolution_convert_fusion.1
  419.9 2.9 copy.34
  422.8 4.4 gather_fusion
  427.2 14.1 %all-to-all-start.2 = ((bf16[16,32,4096]{2,1,0:T(8,128)(2,1)}), bf16[16,32,4096]{2,1,0:T(8,128)(2,1)}, u32[]{:S(2)}, u32[]{:S(2)}) async-start(bf16[16,32,4096]{2,1,0:T(8,128)(2,1)} %bitcast.96), calls=%async_computation.2 | async-start | bytes 8388608 | tf_op jit(solution)/shard_map/all_to_all | solution.py:107
  441.3 0.0 all-reduce.2.cloned.1.call-start
  441.3 97.7 %reduce-scatter.2.cloned.1.call-done = bf16[512,512]{1,0:T(8,128)(2,1)} async-done(((bf16[8192,512]{1,0:T(8,128)(2,1)}), bf16[512,512]{1,0:T(8,128)(2,1)}) %reduce-scatter.2.cloned.1.call-update) | async-done | bytes 524304 | tf_op jit(solution)/shard_map/reduce_scatter | solution.py:112
  539.1 122.4 %all-reduce.2.cloned.1.call-done = bf16[512,512]{1,0:T(8,128)(2,1)} async-done(((bf16[512,512]{1,0:T(8,128)(2,1)}), bf16[512,512]{1,0:T(8,128)(2,1)}) %all-reduce.2.cloned.1.call-update) | async-done | bytes 524304 | tf_op jit(solution)/shard_map/psum | solution.py:120
  661.5 2.1 convert_element_type.61
  663.6 7.4 %gather_fusion.1 = bf16[256,4096]{1,0:T(8,128)(2,1)} fusion(bf16[16,32,4096]{2,1,0:T(8,128)(2,1)} %all-to-all-done.2, s32[256]{0:T(256)S(1)} %bitcast.92), kind=kCustom, calls=%fused_computation.1 | custom fusion | bytes 4196352 | tf_op jit(solution)/shard_map/gather | solution.py:110
  (22 shorter events, 0.2 us)
Async XLA Ops:
  7.2 53.2 %copy-start.2 = (bf16[1,1,256,512]{3,2,1,0:T(8,128)(2,1)S(1)}, bf16[1,1,256,512]{3,2,1,0:T(8,128)(2,1)}, u32[]{:S(2)}) copy-start(bf16[1,1,256,512]{3,2,1,0:T(8,128)(2,1)} %param.13) | copy-start | bytes 786436
  7.2 401.2 %all-gather.3.cloned.1.call-start = ((), (), s32[]{:S(2)}) async-start(), calls=%async_computation.5 | async-start | bytes 8912896 | tf_op jit(solution)/shard_map/all_gather | solution.py:45
  50.5 21.2 %all-to-all-start = ((s32[16,1,32]{2,1,0:T(1,128)}), s32[16,1,32]{2,1,0:T(1,128)S(1)}, u32[]{:S(2)}, u32[]{:S(2)}) async-start(s32[16,1,32]{2,1,0:T(1,128)} %bitcast.8), calls=%async_computation | async-start | bytes 16384 | tf_op jit(solution)/shard_map/all_to_all | solution.py:80
  57.8 6.7 copy-start.3
  68.3 1.7 copy-start.1
  69.5 2.0 copy-start
  75.6 138.5 %all-to-all-start.3 = ((bf16[16,32,512]{2,1,0:T(8,128)(2,1)}), bf16[16,32,512]{2,1,0:T(8,128)(2,1)S(1)}, u32[]{:S(2)}, u32[]{:S(2)}) async-start(bf16[16,32,512]{2,1,0:T(8,128)(2,1)} %bitcast.30), calls=%async_computation.3 | async-start | bytes 1048576 | tf_op jit(solution)/shard_map/all_to_all | solution.py:108
  214.1 7.4 %copy-start.4 = (bf16[512]{0:T(512)(128)(2,1)S(1)}, bf16[512]{0:T(512)(128)(2,1)}, u32[]{:S(2)}) copy-start(bf16[512]{0:T(512)(128)(2,1)} %param.16) | copy-start | bytes 3076
  214.1 174.4 %all-to-all-start.1 = ((bf16[16,32,8192]{2,1,0:T(8,128)(2,1)}), bf16[16,32,8192]{2,1,0:T(8,128)(2,1)}, u32[]{:S(2)}, u32[]{:S(2)}) async-start(bf16[16,32,8192]{2,1,0:T(8,128)(2,1)} %scatter_fusion.1), calls=%async_computation.1 | async-start | bytes 16777216 | tf_op jit(solution)/shard_map/all_to_all | solution.py:79
  221.5 317.6 %reduce-scatter.2.cloned.1.call-start = ((), (), s32[]{:S(2)}) async-start(), calls=%async_computation.6 | async-start | bytes 8912896 | tf_op jit(solution)/shard_map/reduce_scatter | solution.py:112
  427.2 236.4 %all-to-all-start.2 = ((bf16[16,32,4096]{2,1,0:T(8,128)(2,1)}), bf16[16,32,4096]{2,1,0:T(8,128)(2,1)}, u32[]{:S(2)}, u32[]{:S(2)}) async-start(bf16[16,32,4096]{2,1,0:T(8,128)(2,1)} %bitcast.96), calls=%async_computation.2 | async-start | bytes 8388608 | tf_op jit(solution)/shard_map/all_to_all | solution.py:107
  441.3 220.2 %all-reduce.2.cloned.1.call-start = ((), (), s32[]{:S(2)}) async-start(), calls=%async_computation.7 | async-start | bytes 1048576 | tf_op jit(solution)/shard_map/psum | solution.py:120
Sparse Core Ops, SparseCore 0:
  10.4 126.2 all-gather.2
  388.6 150.3 reduce-scatter.1
  541.7 119.7 all-reduce.1
where the time goes:
time: 688 us; the launch traced here: 678 us
  waiting for transfers between devices  221 us (32%)
  local copies, waits for them, and re-layouts  217 us (32%)
  blocking collectives  154 us (22%)
  starting transfers between devices  34.6 us (5%)
  matrix products  22.3 us (3%)
  other arithmetic  15.5 us (2%)
  between operations  14.2 us (2%)
    all_gather x1, blocking collectives, gather_weights(): lax.all_gather(norm_gain, 'fsdp', axis=0, tiled=True)  154 us
    scatter x1, local copies, waits for them, and re-layouts, on_device(): send_rows = jnp.zeros((peer_count, capacity, feature_width), owned.dtype)...  129 us
    psum x1, waiting for transfers between devices, on_device(): gradient = lax.psum(shard_sum, 'dp').astype(jnp.float32)  122 us
    reduce_scatter x1, waiting for transfers between devices, on_device(): lax.psum_scatter(lax.dot_general(normed_own, owner_grad, (((0,), (0,)), (...  97.7 us
    scatter x1, local copies, waits for them, and re-layouts, on_device(): send_positions = jnp.full((peer_count, capacity), row_count, jnp.int32).a...  39 us
    scatter x1, local copies, waits for them, and re-layouts, on_device(): packed = jnp.zeros((row_count, feature_width), owned.dtype).at[landing].s...  16.7 us
    all_to_all x1, starting transfers between devices, on_device(): lax.all_to_all(outgoing, 'dp', split_axis=0, concat_axis=0, tiled=True)  14.1 us
  transfers between devices with their start and end apart: 7, of which 2 were waited for; matrix products, arithmetic and copies ran while one was open for 36% of the time, Pallas kernels for 0%

commit v1 on v0

v1 whole, which is shorter than its diff:
```python
import math

import jax
import jax.numpy as jnp
from jax import lax
from jax.experimental import pallas as pl
from jax.experimental.pallas import tpu as pltpu
from jax.sharding import PartitionSpec as P

HEAD_DIM = 128
HEADS_Q = 32
KV_HEADS = 4
GROUP = HEADS_Q // KV_HEADS
TOK = 256
D = 8192
QW = HEADS_Q * HEAD_DIM
KVW = KV_HEADS * HEAD_DIM
N_DP = 16
N_FSDP = 16
CAP = 32
SLOTS = N_DP * CAP
DSH = D // N_FSDP
DC = DSH // 2
DH = D // 2
EPS = 1e-05
ROWS_X = 128
ROWS_Y = (DC - ROWS_X) // 4
F32 = jnp.float32
BF16 = jnp.bfloat16
MESH = pl.DeviceIdType.MESH
NT = (((1,), (1,)), ((), ()))
TN = (((0,), (0,)), ((), ()))


def dot(a, b):
    return jnp.dot(a, b, preferred_element_type=F32)


def remote(src, dst, send_sem, recv_sem, device):
    return pltpu.make_async_remote_copy(
        src_ref=src, dst_ref=dst, send_sem=send_sem, recv_sem=recv_sem,
        device_id=device, device_id_type=MESH,
    )


def slot_matrices(ids):
    wide = jnp.broadcast_to(ids.astype(F32), (TOK, TOK))
    tall = wide.T
    begin = jnp.sum((tall < wide).astype(F32), axis=0, keepdims=True)
    place = lax.broadcasted_iota(jnp.int32, (1, TOK), 1).astype(F32)
    slot = ids.astype(F32) * CAP + place - begin
    slot_wide = jnp.broadcast_to(slot, (SLOTS, TOK))
    onehot = slot_wide == lax.broadcasted_iota(jnp.int32, (SLOTS, TOK), 0).astype(F32)
    return onehot.astype(F32).astype(BF16)


def kernel(
    rows_ref, target_ref, q_ref, keys_ref, cot_ref, seg_ref, gain_ref, w_ref,
    out_ref, grad_ref,
    r_all, r_other, w_all, q_buf, c_buf, w_buf, qr, cr, kb, pt_s, pt_r, g_s, g_r, g_own,
    gt, a_r, b_r, a2_r, b2_r, a1, b1, s3, r3, fin, v_s, v_r, vb, att, st_ref,
    local_sem, row_s, row_r, wx_s, wx_r, wy_s, wy_r, wx2_s, wx2_r, wy2_s, wy2_r,
    g_ss, g_rs, p_ss, p_rs, go_s, go_r, v_ss, v_rs,
    a_ss, a_rs, b_ss, b_rs, a2_ss, a2_rs, b2_ss, b2_rs, z_ss, z_rs, f_ss, f_rs,
):
    p = lax.axis_index("dp")
    f = lax.axis_index("fsdp")
    zl, y, c = p // 8, (p // 2) % 4, p % 2
    x, zh = f // 4, f % 4
    z = zh * 2 + zl
    sgn = 2 * zl - 1

    def at_z(zz, yy, xx):
        zz = lax.rem(zz + 16, 8)
        return (((zz % 2) * 4 + yy) * 2 + c, xx * 4 + zz // 2)

    def at_x(d):
        return (p, ((x + d) % 4) * 4 + zh)

    def at_y(d):
        return ((zl * 4 + (y + d) % 4) * 2 + c, f)

    sibling = ((zl * 4 + y) * 2 + (1 - c), f)

    loads = [
        pltpu.make_async_copy(w_ref.at[pl.ds(c * DC, DC)], w_buf, local_sem.at[0]),
        pltpu.make_async_copy(q_ref, q_buf, local_sem.at[1]),
        pltpu.make_async_copy(cot_ref, c_buf, local_sem.at[2]),
    ]
    for cp in loads:
        cp.start()

    def row_load(i, half):
        col = pl.multiple_of(i * DSH + half * DC, 128)
        to = pl.multiple_of(i * DC, 128)
        return col, to

    def start_rows(i, _):
        col, to = row_load(i, 1 - c)
        pltpu.make_async_copy(
            rows_ref.at[:, pl.ds(col, DC)], r_other.at[:, pl.ds(to, DC)], local_sem.at[3]
        ).start()
        col, to = row_load(i, c)
        pltpu.make_async_copy(
            rows_ref.at[:, pl.ds(col, DC)], r_all.at[pl.ds(0, TOK), pl.ds(to, DC)], local_sem.at[4]
        ).start()
        return 0

    lax.fori_loop(0, N_FSDP, start_rows, 0)

    barrier = pltpu.get_barrier_semaphore()

    def greet(i, _):
        pl.semaphore_signal(barrier, inc=1, device_id=((p + i) % 16, f), device_id_type=MESH)
        pl.semaphore_signal(barrier, inc=1, device_id=(p, (f + i) % 16), device_id_type=MESH)
        return 0

    lax.fori_loop(1, 16, greet, 0)

    def greet_z(i, _):
        pl.semaphore_signal(
            barrier, inc=1,
            device_id=(((1 - zl) * 4 + y) * 2 + c, x * 4 + (zh + i) % 4), device_id_type=MESH,
        )
        return 0

    lax.fori_loop(1, 4, greet_z, 0)

    def greet_xz(i, _):
        dx, dz = 1 + i // 3, 1 + i % 3
        pl.semaphore_signal(
            barrier, inc=1,
            device_id=(((1 - zl) * 4 + y) * 2 + c, ((x + dx) % 4) * 4 + (zh + dz) % 4),
            device_id_type=MESH,
        )
        return 0

    lax.fori_loop(0, 9, greet_xz, 0)
    pl.semaphore_wait(barrier, 30 + 3 + 9)

    loads[0].wait()
    own_gain = gain_ref[:, pl.ds(pl.multiple_of(c * DC, 128), DC)]
    eye = lax.broadcasted_iota(jnp.int32, (DC, DC), 0) == lax.broadcasted_iota(jnp.int32, (DC, DC), 1)
    diagonal = jnp.where(eye, jnp.broadcast_to(own_gain.astype(F32), (DC, DC)), 0.0).astype(BF16)
    w_all[f] = dot(diagonal, w_buf[...]).astype(BF16)

    y_rows = pl.ds(pl.multiple_of(ROWS_X + y * ROWS_Y, 16), ROWS_Y)

    def wx_copy(k):
        part = w_all.at[f, pl.ds(0, ROWS_X)]
        return remote(part, part, wx_s.at[k - 1], wx_r.at[k - 1], at_z(z + sgn * k, y, x))

    def wy_copy(i):
        part = w_all.at[f, y_rows]
        return remote(part, part, wy_s.at[i], wy_r.at[i], at_z(z + sgn * (i % 4), y, (x + i // 4) % 4))

    for k in (3, 2, 1):
        wx_copy(k).start()

    def start_wy(i, _):
        wy_copy(i).start()
        return 0

    lax.fori_loop(1, 16, start_wy, 0)

    row_copy = remote(r_other, r_all.at[pl.ds(TOK, TOK)], row_s, row_r, sibling)
    pltpu.make_async_copy(r_other, r_other, local_sem.at[3]).wait()
    row_copy.start()

    onehot = slot_matrices(seg_ref[...])
    keys_pad = dot(onehot, keys_ref[...]).astype(BF16).reshape(N_DP, 2, 16, KVW)
    kb[...] = jnp.zeros_like(kb)
    for g in range(KV_HEADS):
        lanes = slice(g * 128, (g + 1) * 128)
        kb[:, :, g, :, lanes] = keys_pad[:, :, :, lanes]
    loads[1].wait()
    loads[2].wait()
    for g in range(KV_HEADS):
        wide = slice(g * 1024, (g + 1) * 1024)
        lanes = slice(g * 128, (g + 1) * 128)
        q_pad = dot(onehot, q_buf[:, wide]).astype(BF16).reshape(N_DP, 2, 16, 1024)
        c_pad = dot(onehot, c_buf[:, wide]).astype(BF16).reshape(N_DP, 2, 16, 1024)
        for s in range(GROUP):
            part = slice(s * 128, (s + 1) * 128)
            qr[:, :, s, :, lanes] = q_pad[:, :, :, part]
            cr[:, :, s, :, lanes] = c_pad[:, :, :, part]

    row_i = lax.broadcasted_iota(jnp.int32, (128, 256), 0)
    col_i = lax.broadcasted_iota(jnp.int32, (128, 256), 1)
    allowed = (row_i // 64) * 16 + row_i % 16 <= (col_i // 128) * 16 + col_i % 16

    def g_copy(o):
        return remote(g_s.at[o], g_r.at[p], g_ss.at[o], g_rs.at[p], (o, f))

    def p_copy(o):
        return remote(pt_s.at[o], pt_r.at[p], p_ss.at[o], p_rs.at[p], (o, f))

    def trainer(o):
        scores = lax.dot_general(
            kb[o].reshape(128, KVW), qr[o].reshape(256, KVW), NT, preferred_element_type=F32
        )
        scores = jnp.where(allowed, scores * (1.0 / math.sqrt(HEAD_DIM)), -1e30)
        scores = scores.reshape(2, 4, 16, 256)
        highest = jnp.max(jnp.max(scores, axis=0, keepdims=True), axis=2, keepdims=True)
        powers = jnp.exp(scores - highest)
        total = jnp.sum(jnp.sum(powers, axis=0, keepdims=True), axis=2, keepdims=True)
        prob = (powers / total).astype(BF16).reshape(128, 256)
        pt_s[o, 0:64] = prob[0:64, 0:128]
        pt_s[o, 64:192] = prob[:, 128:256]
        grad = dot(prob, cr[o].reshape(256, KVW)).astype(BF16)
        for kh in range(2):
            for g in range(KV_HEADS):
                lanes = slice(g * 128, (g + 1) * 128)
                g_s[o, kh * 16:(kh + 1) * 16, lanes] = grad[kh * 64 + g * 16:kh * 64 + (g + 1) * 16, lanes]

    def trainer_step(i, _):
        o = (p + i) % 16
        trainer(o)
        g_copy(o).start()
        return 0

    lax.fori_loop(1, 16, trainer_step, 0)
    trainer(p)
    g_r[p] = g_s[p]
    pt_r[p] = pt_s[p]

    def start_p(i, _):
        p_copy((p + i) % 16).start()
        return 0

    lax.fori_loop(1, 16, start_p, 0)

    def wx2_copy(d):
        part = w_all.at[pl.ds(x * 4, 4), pl.ds(0, ROWS_X)]
        return remote(part, part, wx2_s.at[d - 1], wx2_r.at[d - 1], at_x(d))

    def wy2_copy(d):
        part = w_all.at[:, y_rows]
        return remote(part, part, wy2_s.at[d - 1], wy2_r.at[d - 1], at_y(d))

    for k in (1, 2, 3):
        wx_copy(k).wait_recv()

    pltpu.make_async_copy(r_other, r_other, local_sem.at[4]).wait()

    def square(i, acc):
        col = pl.ds(pl.multiple_of(i * 512, 128), 512)
        own = r_all[0:TOK, col].astype(F32)
        oth = r_other[:, col].astype(F32)
        both = own * own + oth * oth
        return acc + both[:, 0:128] + both[:, 128:256] + both[:, 256:384] + both[:, 384:512]

    squares = lax.fori_loop(0, DH // 512, square, jnp.zeros((TOK, 128), F32))
    inverse = lax.rsqrt(jnp.sum(squares, axis=1, keepdims=True) * (1.0 / D) + EPS)
    owner_hot = slot_matrices(target_ref[...])
    st_ref[...] = owner_hot

    def wait_g(i, _):
        o = (p + i) % 16
        remote(g_s.at[o], g_r.at[o], g_ss.at[o], g_rs.at[o], (o, f)).wait_recv()
        return 0

    lax.fori_loop(1, 16, wait_g, 0)
    owner_grad = lax.dot_general(owner_hot, g_r[...].reshape(SLOTS, KVW), TN, preferred_element_type=F32)
    g_own[0:TOK] = (owner_grad * inverse).astype(BF16)
    go_copy = remote(g_own.at[pl.ds(0, TOK)], g_own.at[pl.ds(TOK, TOK)], go_s, go_r, sibling)
    go_copy.start()
    for d in (2, 1, 3):
        wx2_copy(d).start()
    row_copy.wait()
    go_copy.wait()

    def a_copy(d):
        part = gt.at[pl.ds(0, 256), pl.ds(pl.multiple_of(((x + d) % 4) * 1024, 128), 1024)]
        return remote(part, a_r.at[d - 1], a_ss.at[d - 1], a_rs.at[d - 1], at_x(d))

    def b_copy(d):
        part = gt.at[pl.ds(pl.multiple_of(256 + ((y + d) % 4) * 64, 16), 64)]
        return remote(part, b_r.at[d - 1], b_ss.at[d - 1], b_rs.at[d - 1], at_y(d))

    grad_rows = g_own[...]

    def partial(i, base):
        col = pl.ds(pl.multiple_of(base + i * 512, 128), 512)
        gt[:, col] = lax.dot_general(grad_rows, r_all[:, col], TN, preferred_element_type=F32).astype(BF16)
        return base

    for d in (2, 1, 3, 0):
        lax.fori_loop(0, 2, partial, ((x + d) % 4) * 1024)
        if d:
            a_copy(d).start()
    for d in (2, 1, 3):
        b_copy(d).start()

    def wait_wy(i, _):
        wy_copy(i).wait_recv()
        return 0

    lax.fori_loop(1, 16, wait_wy, 0)
    for d in (2, 1, 3):
        wy2_copy(d).start()

    for d in (1, 2, 3):
        a_copy(d).wait_recv()
    own_cols = pl.ds(pl.multiple_of(x * 1024, 128), 1024)
    a1[...] = (
        gt[0:256, own_cols].astype(F32) + a_r[0].astype(F32) + a_r[1].astype(F32) + a_r[2].astype(F32)
    ).astype(BF16)

    def a2_copy(d):
        part = a1.at[pl.ds(pl.multiple_of(((y + d) % 4) * 64, 16), 64)]
        return remote(part, a2_r.at[d - 1], a2_ss.at[d - 1], a2_rs.at[d - 1], at_y(d))

    for d in (2, 1, 3):
        a2_copy(d).start()
    for d in (1, 2, 3):
        b_copy(d).wait_recv()
    own_rows = pl.ds(pl.multiple_of(256 + y * 64, 16), 64)
    b1[...] = (
        gt[own_rows].astype(F32) + b_r[0].astype(F32) + b_r[1].astype(F32) + b_r[2].astype(F32)
    ).astype(BF16)

    def b2_copy(d):
        part = b1.at[:, pl.ds(pl.multiple_of(((x + d) % 4) * 1024, 128), 1024)]
        return remote(part, b2_r.at[d - 1], b2_ss.at[d - 1], b2_rs.at[d - 1], at_x(d))

    for d in (2, 1, 3):
        b2_copy(d).start()

    for d in (1, 2, 3):
        wx2_copy(d).wait_recv()
        wy2_copy(d).wait_recv()

    def project(i, acc):
        return acc + dot(r_all[:, pl.ds(pl.multiple_of(i * DC, 128), DC)], w_all[i])

    v_s[...] = lax.fori_loop(0, N_FSDP, project, jnp.zeros((2 * TOK, KVW), F32))
    v_copy = remote(v_s.at[pl.ds(TOK, TOK)], v_r, v_ss, v_rs, sibling)
    v_copy.start()

    for d in (1, 2, 3):
        a2_copy(d).wait_recv()
    own_a = pl.ds(pl.multiple_of(y * 64, 16), 64)
    s3[0] = (
        a1[own_a].astype(F32) + a2_r[0].astype(F32) + a2_r[1].astype(F32) + a2_r[2].astype(F32)
    ).astype(BF16)
    for d in (1, 2, 3):
        b2_copy(d).wait_recv()
    s3[1] = (
        b1[:, own_cols].astype(F32) + b2_r[0].astype(F32) + b2_r[1].astype(F32) + b2_r[2].astype(F32)
    ).astype(BF16)

    def z_part(zz):
        zz = lax.rem(zz, 8)
        return s3.at[
            :, pl.ds(pl.multiple_of((zz % 2) * 32, 16), 32), pl.ds(pl.multiple_of((zz // 2) * DC, 128), DC)
        ]

    def z_copy(k):
        return remote(z_part(z + k), r3.at[k - 1], z_ss.at[k - 1], z_rs.at[k - 1], at_z(z + k, y, x))

    for k in (4, 3, 5, 2, 6, 1, 7):
        z_copy(k).start()

    v_copy.wait()
    values = ((v_s[0:TOK] + v_r[...]) * inverse).astype(BF16)
    values_pad = dot(st_ref[...], values).astype(BF16).reshape(N_DP, 2, 16, KVW)
    vb[...] = jnp.zeros_like(vb)
    for g in range(KV_HEADS):
        lanes = slice(g * 128, (g + 1) * 128)
        vb[:, :, g, :, lanes] = values_pad[:, :, :, lanes]

    for k in range(1, 8):
        z_copy(k).wait_recv()
    total = z_part(z)[...].astype(F32)
    for k in range(7):
        total = total + r3[k].astype(F32)
    fin[p] = (total * own_gain.astype(F32).reshape(1, 1, DC)).astype(BF16)

    def f_copy(i):
        return remote(fin.at[p], fin.at[p], f_ss.at[i - 1], f_rs.at[i - 1], ((p + i) % 16, f))

    def start_f(i, _):
        f_copy(i).start()
        return 0

    lax.fori_loop(1, 16, start_f, 0)

    def wait_p(i, _):
        o = (p + i) % 16
        remote(pt_s.at[o], pt_r.at[o], p_ss.at[o], p_rs.at[o], (o, f)).wait_recv()
        return 0

    lax.fori_loop(1, 16, wait_p, 0)

    def attend(t, _):
        v_t = vb[t].reshape(128, KVW)
        low = lax.dot_general(pt_r[t, 0:64], v_t[0:64], TN, preferred_element_type=F32).astype(BF16)
        high = lax.dot_general(pt_r[t, 64:192], v_t, TN, preferred_element_type=F32).astype(BF16)
        for half, part in ((0, low), (1, high)):
            for s in range(GROUP):
                for g in range(KV_HEADS):
                    lane = g * 1024 + s * 128
                    att[t, half * 16:(half + 1) * 16, lane:lane + 128] = (
                        part[s * 16:(s + 1) * 16, g * 128:(g + 1) * 128]
                    )
        return 0

    lax.fori_loop(0, N_DP, attend, 0)

    def place(i, _):
        col = pl.ds(pl.multiple_of(i * 512, 128), 512)
        out_ref[:, col] = lax.dot_general(
            st_ref[...], att[:, :, col].reshape(SLOTS, 512), TN, preferred_element_type=F32
        ).astype(BF16)
        return 0

    lax.fori_loop(0, QW // 512, place, 0)

    def wait_f(i, _):
        f_copy(i).wait_recv()
        return 0

    lax.fori_loop(1, 16, wait_f, 0)
    for core in range(2):
        for portion in range(2):
            pieces = []
            for yy in range(4):
                for zz in range(2):
                    pieces.append(fin[(zz * 4 + yy) * 2 + core, portion].astype(F32))
            tall = jnp.concatenate(pieces, axis=0)
            grad_ref[core * DC:(core + 1) * DC, portion * 256:(portion + 1) * 256] = tall.T

    for k in (1, 2, 3):
        wx_copy(k).wait_send()
        wx2_copy(k).wait_send()
        wy2_copy(k).wait_send()
        a_copy(k).wait_send()
        b_copy(k).wait_send()
        a2_copy(k).wait_send()
        b2_copy(k).wait_send()
    for k in range(1, 8):
        z_copy(k).wait_send()

    def wait_sends(i, _):
        wy_copy(i).wait_send()
        g_copy((p + i) % 16).wait_send()
        p_copy((p + i) % 16).wait_send()
        f_copy(i).wait_send()
        return 0

    lax.fori_loop(1, 16, wait_sends, 0)


def on_device(rows_owned, target, offset, queries, keys, cotangent, segment, norm_gain, value_weight):
    dma = pltpu.SemaphoreType.DMA
    vmem = pltpu.VMEM
    scratch = [
        vmem((2 * TOK, DH), BF16),
        vmem((TOK, DH), BF16),
        vmem((N_FSDP, DC, KVW), BF16),
        vmem((TOK, QW), BF16),
        vmem((TOK, QW), BF16),
        vmem((DC, KVW), BF16),
        vmem((N_DP, 2, GROUP, 16, KVW), BF16),
        vmem((N_DP, 2, GROUP, 16, KVW), BF16),
        vmem((N_DP, 2, KV_HEADS, 16, KVW), BF16),
        vmem((N_DP, 192, 128), BF16),
        vmem((N_DP, 192, 128), BF16),
        vmem((N_DP, CAP, KVW), BF16),
        vmem((N_DP, CAP, KVW), BF16),
        vmem((2 * TOK, KVW), BF16),
        vmem((KVW, DH), BF16),
        vmem((3, 256, 1024), BF16),
        vmem((3, 64, DH), BF16),
        vmem((3, 64, 1024), BF16),
        vmem((3, 64, 1024), BF16),
        vmem((256, 1024), BF16),
        vmem((64, DH), BF16),
        vmem((2, 64, 1024), BF16),
        vmem((7, 2, 32, DC), BF16),
        vmem((N_DP, 2, 32, DC), BF16),
        vmem((2 * TOK, KVW), F32),
        vmem((TOK, KVW), F32),
        vmem((N_DP, 2, KV_HEADS, 16, KVW), BF16),
        vmem((N_DP, CAP, QW), BF16),
        vmem((SLOTS, TOK), BF16),
        dma((5,)),
        dma, dma,
        dma((3,)), dma((3,)), dma((16,)), dma((16,)),
        dma((3,)), dma((3,)), dma((3,)), dma((3,)),
        dma((16,)), dma((16,)), dma((16,)), dma((16,)),
        dma, dma, dma, dma,
        dma((3,)), dma((3,)), dma((3,)), dma((3,)),
        dma((3,)), dma((3,)), dma((3,)), dma((3,)),
        dma((7,)), dma((7,)), dma((15,)), dma((15,)),
    ]
    anywhere = pl.BlockSpec(memory_space=pl.ANY)
    inside = pl.BlockSpec(memory_space=pltpu.VMEM)
    returned, gradient = pl.pallas_call(
        kernel,
        out_shape=(
            jax.ShapeDtypeStruct((TOK, QW), BF16),
            jax.ShapeDtypeStruct((DSH, KVW), F32),
        ),
        in_specs=[anywhere, inside, anywhere, inside, anywhere, inside, inside, anywhere],
        out_specs=(inside, inside),
        scratch_shapes=scratch,
        compiler_params=pltpu.CompilerParams(
            collective_id=0, has_side_effects=True, vmem_limit_bytes=60 * 2**20
        ),
        cost_estimate=pl.CostEstimate(flops=8 * 10**9, bytes_accessed=16 * 2**20, transcendentals=10**6),
        name="value_path",
    )(
        rows_owned.reshape(TOK, D),
        target.reshape(1, TOK),
        queries.reshape(TOK, QW),
        keys.reshape(TOK, KVW),
        cotangent.reshape(TOK, QW),
        segment.reshape(1, TOK),
        norm_gain.reshape(1, DSH),
        value_weight,
    )
    return (returned.reshape(1, 1, TOK, QW), gradient)


def solution(mesh):
    placed = (
        P("dp", "fsdp", None, None),
        P("dp", "fsdp", None),
        P("dp", "fsdp", None),
        P("dp", "fsdp", None, None),
        P("dp", "fsdp", None, None),
        P("dp", "fsdp", None, None),
        P("dp", "fsdp", None),
        P("fsdp"),
        P("fsdp", None),
    )
    return jax.shard_map(
        on_device,
        mesh=mesh,
        in_specs=placed,
        out_specs=(P("dp", "fsdp", None, None), P("fsdp", None)),
        check_vma=False,
    )
```

time: 688 us -> 118 us (0.17); the launches traced: 678 us -> 117 us
  waiting for transfers between devices: 221 us -> 0 us
  local copies, waits for them, and re-layouts: 217 us -> 5.45 us
  blocking collectives: 154 us -> 0 us
  Pallas kernels: 0 us -> 111 us
  starting transfers between devices: 34.6 us -> 0 us
  matrix products: 22.3 us -> 0 us
  other arithmetic: 15.5 us -> 0 us
  between operations: 14.2 us -> 0.65 us
    scatter x3 -> x0, local copies, waits for them, and re-layouts: 184 us -> none  [the longest x1 129 us: on_device(): send_rows = jnp.zeros((peer_count, capacity, feature_width), owned.dtype)...]
    all_gather x1 -> x0, blocking collectives: 154 us -> none  [gather_weights(): lax.all_gather(norm_gain, 'fsdp', axis=0, tiled=True)]
    psum x1 -> x0, waiting for transfers between devices: 122 us -> none  [on_device(): gradient = lax.psum(shard_sum, 'dp').astype(jnp.float32)]
    pallas_call x0 -> x1, Pallas kernels: none -> 111 us  [on_device(): pl.pallas_call(kernel, out_shape=(jax.ShapeDtypeStruct((TOK, QW), BF16),...]
    reduce_scatter x1 -> x0, waiting for transfers between devices: 97.7 us -> none  [on_device(): lax.psum_scatter(lax.dot_general(normed_own, owner_grad, (((0,), (0,)), (...]
    all_to_all x4 -> x0, starting transfers between devices: 34.5 us -> none  [the longest x1 14.1 us: on_device(): lax.all_to_all(outgoing, 'dp', split_axis=0, concat_axis=0, tiled=True)]
    dot_general x5 -> x0, matrix products: 22.3 us -> none  [the longest x1 8.15 us: on_device(): lax.dot_general(normed_own, owner_grad, (((0,), (0,)), ((), ())), preferr...]
    gather x4 -> x0, local copies, waits for them, and re-layouts: 16.6 us -> none  [the longest x1 7.44 us: on_device(): returned[targets, slot_index].reshape(1, 1, row_count, HEADS_Q * HEAD_DIM)]
  transfers between devices with their start and end apart: 7 -> 0, of which waited for: 2 -> 0; matrix products, arithmetic and copies ran while one was open for 36% -> 0% of each run, Pallas kernels for 0% -> 0%
where the time goes in v1:
time: 118 us; the launch traced here: 117 us
  Pallas kernels  111 us (94%)
  local copies, waits for them, and re-layouts  5.45 us (5%)
    pallas_call x1, Pallas kernels, on_device(): pl.pallas_call(kernel, out_shape=(jax.ShapeDtypeStruct((TOK, QW), BF16),...  111 us
    unnamed x4, local copies, waits for them, and re-layouts  4.19 us

profile of v1, /device:TPU:1, one launch (start us, length us, event | category | flops | bytes accessed | tf_op | source)
XLA Modules:
  0.0 117.5 jit_solution(15513947909602013923)
XLA Ops:
  0.6 1.3 %reshape.34.gain_ref = bf16[1,512]{1,0:T(2,128)(2,1)} reshape(bf16[512]{0:T(512)(128)(2,1)} %param.15) | data formatting | bytes 2048 | tf_op jit(solution)/shard_map/reshape | solution.py:521
  1.9 111.4 %value_path.1 = (bf16[256,4096]{1,0:T(8,128)(2,1)}, f32[512,512]{1,0:T(8,128)}) custom-call(bf16[256,8192]{1,0:T(8,128)(2,1)} %bitcast.8, s32[1,256]{1,0:T(1,128)} %bitcast.12, bf16[256,4096]{1,0:T(8,128)(2,1)} %bitcast.9, bf16[256,512]{1,0:T(8,128)(2,1)} %bitcast.11, bf16[256,4096]{1,0:T(8,128)(2,1)} %bitcast.10, s32[1,256]{1,0:T(1,128)} %bitcast.13, ...), custom_call_target="tpu_custom_call" | custom-call | flops 8000000000 | bytes 16777216 | tf_op jit(solution)/shard_map/value_path/pallas_call | solution.py:500
  113.3 0.0 copy-start
  113.3 3.2 %copy.12 = bf16[1,1,256,4096]{3,2,1,0:T(8,128)(2,1)} copy(bf16[1,1,256,4096]{3,2,1,0:T(8,128)(2,1)} %bitcast.7) | data formatting | bytes 4194304
  116.5 0.0 copy-done
  116.5 1.0 copy.13
Async XLA Ops:
  113.3 3.2 %copy-start = (f32[512,512]{1,0:T(8,128)S(1)}, f32[512,512]{1,0:T(8,128)}, u32[]{:S(2)}) copy-start(f32[512,512]{1,0:T(8,128)} %get-tuple-element.9) | copy-start | bytes 3145732

commit v2 on v1

--- a/solution.py
+++ b/solution.py
@@ -23,7 +23,10 @@
 DC = DSH // 2
 DH = D // 2
 EPS = 1e-05
-ROWS_X = 128
+ROWS_X = 192
+CHUNKS = 2
+TRAIN = 3
+ROWS_C = ROWS_X // CHUNKS
 ROWS_Y = (DC - ROWS_X) // 4
 F32 = jnp.float32
 BF16 = jnp.bfloat16
@@ -43,7 +46,7 @@
     )
 
 
-def slot_matrices(ids):
+def slot_matrix(ids, tall_too=False):
     wide = jnp.broadcast_to(ids.astype(F32), (TOK, TOK))
     tall = wide.T
     begin = jnp.sum((tall < wide).astype(F32), axis=0, keepdims=True)
@@ -51,14 +54,85 @@
     slot = ids.astype(F32) * CAP + place - begin
     slot_wide = jnp.broadcast_to(slot, (SLOTS, TOK))
     onehot = slot_wide == lax.broadcasted_iota(jnp.int32, (SLOTS, TOK), 0).astype(F32)
-    return onehot.astype(F32).astype(BF16)
+    onehot = onehot.astype(F32).astype(BF16)
+    if not tall_too:
+        return onehot
+    slot_tall = jnp.broadcast_to(slot, (TOK, TOK)).T
+    slot_tall = jnp.concatenate([slot_tall] * (SLOTS // TOK), axis=1)
+    flipped = slot_tall == lax.broadcasted_iota(jnp.int32, (TOK, SLOTS), 1).astype(F32)
+    return onehot, flipped.astype(F32).astype(BF16)
+
+
+class RingGather:
+    def __init__(self, part, me, device, send, recv, base=0):
+        self.part, self.me, self.device = part, me, device
+        self.send, self.recv, self.base = send, recv, base
+
+    def copy(self, i):
+        place, half, way = (
+            (0, 0, 1), (0, 1, 1), (0, 1, -1), (0, 0, -1), (-1, 0, 1), (1, 1, -1)
+        )[i]
+        part = self.part((self.me + place) % 4, half)
+        return remote(
+            part, part, self.send.at[self.base + i], self.recv.at[self.base + i], self.device(way)
+        )
+
+    def start(self):
+        for i in (0, 2, 1, 3):
+            self.copy(i).start()
+
+    def forward(self):
+        for i in (0, 2):
+            self.copy(i).wait_recv()
+            self.copy(4 + i // 2).start()
+
+    def finish(self):
+        for i in (1, 3, 4, 5):
+            self.copy(i).wait_recv()
+
+    def wait_send(self):
+        for i in range(6):
+            self.copy(i).wait_send()
+
+
+class RingReduce:
+    def __init__(self, part, me, device, via, near, send, recv):
+        self.part, self.me, self.device = part, me, device
+        self.via, self.near, self.send, self.recv = via, near, send, recv
+
+    def copy(self, i):
+        place, half, way = ((2, 0, 1), (2, 1, -1), (1, 1, 1), (-1, 0, -1), (1, 0, 1), (-1, 1, -1))[i]
+        to = self.via.at[half] if i < 2 else self.near.at[0 if way == 1 else 1, half]
+        return remote(
+            self.part((self.me + place) % 4, half), to, self.send.at[i], self.recv.at[i], self.device(way)
+        )
+
+    def forward(self):
+        for half, place in ((0, 1), (1, -1)):
+            self.copy(half).wait_recv()
+            part = self.part((self.me + place) % 4, half)
+            part[...] = (part[...].astype(F32) + self.via[half].astype(F32)).astype(BF16)
+            self.copy(4 + half).start()
+
+    def finish(self):
+        for i in range(2, 6):
+            self.copy(i).wait_recv()
+
+    def total(self, half):
+        own = self.part(self.me, half)[...].astype(F32)
+        return own + self.near[0, half].astype(F32) + self.near[1, half].astype(F32)
+
+    def wait_send(self):
+        for i in range(6):
+            self.copy(i).wait_send()
 
 
 def kernel(
     rows_ref, target_ref, q_ref, keys_ref, cot_ref, seg_ref, gain_ref, w_ref,
     out_ref, grad_ref,
     r_all, r_other, w_all, q_buf, c_buf, w_buf, qr, cr, kb, pt_s, pt_r, g_s, g_r, g_own,
-    gt, a_r, b_r, a2_r, b2_r, a1, b1, s3, r3, fin, v_s, v_r, vb, att, st_ref,
+    gt, a_via, a_near, b_via, b_near, a2_r, b2_r, a1, b1, s3, r3, fin, v_s, v_r, vb, att, st_ref,
+    ft_ref, gw,
     local_sem, row_s, row_r, wx_s, wx_r, wy_s, wy_r, wx2_s, wx2_r, wy2_s, wy2_r,
     g_ss, g_rs, p_ss, p_rs, go_s, go_r, v_ss, v_rs,
     a_ss, a_rs, b_ss, b_rs, a2_ss, a2_rs, b2_ss, b2_rs, z_ss, z_rs, f_ss, f_rs,
@@ -117,17 +191,8 @@
 
     lax.fori_loop(1, 16, greet, 0)
 
-    def greet_z(i, _):
-        pl.semaphore_signal(
-            barrier, inc=1,
-            device_id=(((1 - zl) * 4 + y) * 2 + c, x * 4 + (zh + i) % 4), device_id_type=MESH,
-        )
-        return 0
-
-    lax.fori_loop(1, 4, greet_z, 0)
-
-    def greet_xz(i, _):
-        dx, dz = 1 + i // 3, 1 + i % 3
+    def greet_other(i, _):
+        dx, dz = i // 3, 1 + i % 3
         pl.semaphore_signal(
             barrier, inc=1,
             device_id=(((1 - zl) * 4 + y) * 2 + c, ((x + dx) % 4) * 4 + (zh + dz) % 4),
@@ -135,27 +200,30 @@
         )
         return 0
 
-    lax.fori_loop(0, 9, greet_xz, 0)
-    pl.semaphore_wait(barrier, 30 + 3 + 9)
+    lax.fori_loop(0, 12, greet_other, 0)
 
     loads[0].wait()
     own_gain = gain_ref[:, pl.ds(pl.multiple_of(c * DC, 128), DC)]
     eye = lax.broadcasted_iota(jnp.int32, (DC, DC), 0) == lax.broadcasted_iota(jnp.int32, (DC, DC), 1)
     diagonal = jnp.where(eye, jnp.broadcast_to(own_gain.astype(F32), (DC, DC)), 0.0).astype(BF16)
     w_all[f] = dot(diagonal, w_buf[...]).astype(BF16)
+    onehot = slot_matrix(seg_ref[...])
+    pl.semaphore_wait(barrier, 30 + 12)
 
     y_rows = pl.ds(pl.multiple_of(ROWS_X + y * ROWS_Y, 16), ROWS_Y)
 
-    def wx_copy(k):
-        part = w_all.at[f, pl.ds(0, ROWS_X)]
-        return remote(part, part, wx_s.at[k - 1], wx_r.at[k - 1], at_z(z + sgn * k, y, x))
+    def wx_copy(j, k):
+        part = w_all.at[f, pl.ds(j * ROWS_C, ROWS_C)]
+        i = j * 3 + k - 1
+        return remote(part, part, wx_s.at[i], wx_r.at[i], at_z(z + sgn * k, y, x))
 
     def wy_copy(i):
         part = w_all.at[f, y_rows]
         return remote(part, part, wy_s.at[i], wy_r.at[i], at_z(z + sgn * (i % 4), y, (x + i // 4) % 4))
 
-    for k in (3, 2, 1):
-        wx_copy(k).start()
+    for j in range(CHUNKS):
+        for k in (3, 2, 1):
+            wx_copy(j, k).start()
 
     def start_wy(i, _):
         wy_copy(i).start()
@@ -167,7 +235,6 @@
     pltpu.make_async_copy(r_other, r_other, local_sem.at[3]).wait()
     row_copy.start()
 
-    onehot = slot_matrices(seg_ref[...])
     keys_pad = dot(onehot, keys_ref[...]).astype(BF16).reshape(N_DP, 2, 16, KVW)
     kb[...] = jnp.zeros_like(kb)
     for g in range(KV_HEADS):
@@ -195,32 +262,62 @@
     def p_copy(o):
         return remote(pt_s.at[o], pt_r.at[p], p_ss.at[o], p_rs.at[p], (o, f))
 
-    def trainer(o):
-        scores = lax.dot_general(
-            kb[o].reshape(128, KVW), qr[o].reshape(256, KVW), NT, preferred_element_type=F32
-        )
-        scores = jnp.where(allowed, scores * (1.0 / math.sqrt(HEAD_DIM)), -1e30)
-        scores = scores.reshape(2, 4, 16, 256)
-        highest = jnp.max(jnp.max(scores, axis=0, keepdims=True), axis=2, keepdims=True)
-        powers = jnp.exp(scores - highest)
-        total = jnp.sum(jnp.sum(powers, axis=0, keepdims=True), axis=2, keepdims=True)
-        prob = (powers / total).astype(BF16).reshape(128, 256)
-        pt_s[o, 0:64] = prob[0:64, 0:128]
-        pt_s[o, 64:192] = prob[:, 128:256]
-        grad = dot(prob, cr[o].reshape(256, KVW)).astype(BF16)
-        for kh in range(2):
-            for g in range(KV_HEADS):
-                lanes = slice(g * 128, (g + 1) * 128)
-                g_s[o, kh * 16:(kh + 1) * 16, lanes] = grad[kh * 64 + g * 16:kh * 64 + (g + 1) * 16, lanes]
+    def trainer(owners):
+        scores = [
+            lax.dot_general(
+                kb[o].reshape(128, KVW), qr[o].reshape(256, KVW), NT, preferred_element_type=F32
+            )
+            for o in owners
+        ]
+        probs = []
+        for o, score in zip(owners, scores):
+            score = jnp.where(allowed, score * (1.0 / math.sqrt(HEAD_DIM)), -1e30)
+            score = score.reshape(2, 4, 16, 256)
+            highest = jnp.max(jnp.max(score, axis=0, keepdims=True), axis=2, keepdims=True)
+            powers = jnp.exp(score - highest)
+            total = jnp.sum(jnp.sum(powers, axis=0, keepdims=True), axis=2, keepdims=True)
+            probs.append((powers / total).astype(BF16).reshape(128, 256))
+        for o, prob in zip(owners, probs):
+            grad = dot(prob, cr[o].reshape(256, KVW)).astype(BF16)
+            for kh in range(2):
+                for g in range(KV_HEADS):
+                    lanes = slice(g * 128, (g + 1) * 128)
+                    g_s[o, kh * 16:(kh + 1) * 16, lanes] = (
+                        grad[kh * 64 + g * 16:kh * 64 + (g + 1) * 16, lanes]
+                    )
+            pt_s[o, 0:64] = prob[0:64, 0:128]
+            pt_s[o, 64:192] = prob[:, 128:256]
+
+    def x_part(j):
+        def part(xx, half):
+            return w_all.at[pl.ds(xx * 4, 4), pl.ds(j * ROWS_C + half * (ROWS_C // 2), ROWS_C // 2)]
+
+        return part
+
+    wx2 = [RingGather(x_part(j), x, at_x, wx2_s, wx2_r, 6 * j) for j in range(CHUNKS)]
+
+    def y_part(yy, half):
+        rows = pl.ds(pl.multiple_of(ROWS_X + yy * ROWS_Y, 16), ROWS_Y)
+        return w_all.at[pl.ds(half * 8, 8), rows]
+
+    wy2 = RingGather(y_part, y, at_y, wy2_s, wy2_r)
 
     def trainer_step(i, _):
-        o = (p + i) % 16
-        trainer(o)
-        g_copy(o).start()
-        return 0
-
-    lax.fori_loop(1, 16, trainer_step, 0)
-    trainer(p)
+        owners = [(p + 1 + i * TRAIN + j) % 16 for j in range(TRAIN)]
+        trainer(owners)
+        for o in owners:
+            g_copy(o).start()
+
+        @pl.when(i == 1)
+        def _():
+            for k in (1, 2, 3):
+                wx_copy(0, k).wait_recv()
+            wx2[0].start()
+
+        return 0
+
+    lax.fori_loop(0, 15 // TRAIN, trainer_step, 0)
+    trainer([p])
     g_r[p] = g_s[p]
     pt_r[p] = pt_s[p]
 
@@ -229,17 +326,10 @@
         return 0
 
     lax.fori_loop(1, 16, start_p, 0)
-
-    def wx2_copy(d):
-        part = w_all.at[pl.ds(x * 4, 4), pl.ds(0, ROWS_X)]
-        return remote(part, part, wx2_s.at[d - 1], wx2_r.at[d - 1], at_x(d))
-
-    def wy2_copy(d):
-        part = w_all.at[:, y_rows]
-        return remote(part, part, wy2_s.at[d - 1], wy2_r.at[d - 1], at_y(d))
-
     for k in (1, 2, 3):
-        wx_copy(k).wait_recv()
+        wx_copy(1, k).wait_recv()
+    wx2[0].forward()
+    wx2[1].start()
 
     pltpu.make_async_copy(r_other, r_other, local_sem.at[4]).wait()
 
@@ -252,8 +342,9 @@
 
     squares = lax.fori_loop(0, DH // 512, square, jnp.zeros((TOK, 128), F32))
     inverse = lax.rsqrt(jnp.sum(squares, axis=1, keepdims=True) * (1.0 / D) + EPS)
-    owner_hot = slot_matrices(target_ref[...])
+    owner_hot, owner_tall = slot_matrix(target_ref[...], True)
     st_ref[...] = owner_hot
+    ft_ref[...] = owner_tall
 
     def wait_g(i, _):
         o = (p + i) % 16
@@ -261,51 +352,74 @@
         return 0
 
     lax.fori_loop(1, 16, wait_g, 0)
-    owner_grad = lax.dot_general(owner_hot, g_r[...].reshape(SLOTS, KVW), TN, preferred_element_type=F32)
+    owner_grad = dot(owner_tall, g_r[...].reshape(SLOTS, KVW))
     g_own[0:TOK] = (owner_grad * inverse).astype(BF16)
     go_copy = remote(g_own.at[pl.ds(0, TOK)], g_own.at[pl.ds(TOK, TOK)], go_s, go_r, sibling)
     go_copy.start()
-    for d in (2, 1, 3):
-        wx2_copy(d).start()
     row_copy.wait()
-    go_copy.wait()
-
-    def a_copy(d):
-        part = gt.at[pl.ds(0, 256), pl.ds(pl.multiple_of(((x + d) % 4) * 1024, 128), 1024)]
-        return remote(part, a_r.at[d - 1], a_ss.at[d - 1], a_rs.at[d - 1], at_x(d))
-
-    def b_copy(d):
-        part = gt.at[pl.ds(pl.multiple_of(256 + ((y + d) % 4) * 64, 16), 64)]
-        return remote(part, b_r.at[d - 1], b_ss.at[d - 1], b_rs.at[d - 1], at_y(d))
-
-    grad_rows = g_own[...]
-
-    def partial(i, base):
-        col = pl.ds(pl.multiple_of(base + i * 512, 128), 512)
-        gt[:, col] = lax.dot_general(grad_rows, r_all[:, col], TN, preferred_element_type=F32).astype(BF16)
-        return base
-
-    for d in (2, 1, 3, 0):
-        lax.fori_loop(0, 2, partial, ((x + d) % 4) * 1024)
-        if d:
-            a_copy(d).start()
-    for d in (2, 1, 3):
-        b_copy(d).start()
 
     def wait_wy(i, _):
         wy_copy(i).wait_recv()
         return 0
 
     lax.fori_loop(1, 16, wait_wy, 0)
-    for d in (2, 1, 3):
-        wy2_copy(d).start()
-
-    for d in (1, 2, 3):
-        a_copy(d).wait_recv()
-    own_cols = pl.ds(pl.multiple_of(x * 1024, 128), 1024)
-    a1[...] = (
-        gt[0:256, own_cols].astype(F32) + a_r[0].astype(F32) + a_r[1].astype(F32) + a_r[2].astype(F32)
-    ).astype(BF16)
+    wy2.start()
+    go_copy.wait()
+
+    def a_part(xx, half):
+        return gt.at[pl.ds(half * 128, 128), pl.ds(pl.multiple_of(xx * 1024, 128), 1024)]
+
+    def b_part(yy, half):
+        return gt.at[pl.ds(pl.multiple_of(256 + yy * 64 + half * 32, 16), 32)]
+
+    ring_a = RingReduce(a_part, x, at_x, a_via, a_near, a_ss, a_rs)
+    ring_b = RingReduce(b_part, y, at_y, b_via, b_near, b_ss, b_rs)
+    gw[...] = g_own[...].T
+
+    def partial(portion):
+        def step(i, base):
+            col = pl.ds(pl.multiple_of(base + i * 512, 128), 512)
+            rows = slice(portion * 256, (portion + 1) * 256)
+            gt[rows, col] = dot(gw[rows], r_all[:, col]).astype(BF16)
+            return base
+
+        return step
+
+    def partial_a(d):
+        lax.fori_loop(0, 2, partial(0), ((x + d) % 4) * 1024)
+
+    partial_a(2)
+    ring_a.copy(0).start()
+    ring_a.copy(1).start()
+    lax.fori_loop(0, 8, partial(1), 0)
+    for i in (0, 1, 2, 3):
+        ring_b.copy(i).start()
+    partial_a(1)
+    ring_a.copy(2).start()
+    partial_a(3)
+    ring_a.copy(3).start()
+    partial_a(0)
+
+    wx2[1].forward()
+    wy2.forward()
+
+    ring_a.forward()
+    ring_b.forward()
+
+    for ring in (wx2[0], wx2[1], wy2):
+        ring.finish()
+    for m in (1, 0):
+        for n in range(2):
+            cols = slice(n * 256, (n + 1) * 256)
+            rows = slice(m * TOK, (m + 1) * TOK)
+            v_s[rows, cols] = dot(r_all[rows], w_all[:, :, cols].reshape(DH, 256))
+        if m == 1:
+            v_copy = remote(v_s.at[pl.ds(TOK, TOK)], v_r, v_ss, v_rs, sibling)
+            v_copy.start()
+
+    ring_a.finish()
+    for half in range(2):
+        a1[half * 128:(half + 1) * 128] = ring_a.total(half).astype(BF16)
 
     def a2_copy(d):
         part = a1.at[pl.ds(pl.multiple_of(((y + d) % 4) * 64, 16), 64)]
@@ -313,12 +427,9 @@
 
     for d in (2, 1, 3):
         a2_copy(d).start()
-    for d in (1, 2, 3):
-        b_copy(d).wait_recv()
-    own_rows = pl.ds(pl.multiple_of(256 + y * 64, 16), 64)
-    b1[...] = (
-        gt[own_rows].astype(F32) + b_r[0].astype(F32) + b_r[1].astype(F32) + b_r[2].astype(F32)
-    ).astype(BF16)
+    ring_b.finish()
+    for half in range(2):
+        b1[half * 32:(half + 1) * 32] = ring_b.total(half).astype(BF16)
 
     def b2_copy(d):
         part = b1.at[:, pl.ds(pl.multiple_of(((x + d) % 4) * 1024, 128), 1024)]
@@ -327,20 +438,41 @@
     for d in (2, 1, 3):
         b2_copy(d).start()
 
-    for d in (1, 2, 3):
-        wx2_copy(d).wait_recv()
-        wy2_copy(d).wait_recv()
-
-    def project(i, acc):
-        return acc + dot(r_all[:, pl.ds(pl.multiple_of(i * DC, 128), DC)], w_all[i])
-
-    v_s[...] = lax.fori_loop(0, N_FSDP, project, jnp.zeros((2 * TOK, KVW), F32))
-    v_copy = remote(v_s.at[pl.ds(TOK, TOK)], v_r, v_ss, v_rs, sibling)
-    v_copy.start()
+    v_copy.wait()
+    values = ((v_s[0:TOK] + v_r[...]) * inverse).astype(BF16)
+    values_pad = dot(st_ref[...], values).astype(BF16).reshape(N_DP, 2, 16, KVW)
+    vb[...] = jnp.zeros_like(vb)
+    for g in range(KV_HEADS):
+        lanes = slice(g * 128, (g + 1) * 128)
+        vb[:, :, g, :, lanes] = values_pad[:, :, :, lanes]
+
+    def wait_p(i, _):
+        o = (p + i) % 16
+        remote(pt_s.at[o], pt_r.at[o], p_ss.at[o], p_rs.at[o], (o, f)).wait_recv()
+        return 0
+
+    lax.fori_loop(1, 16, wait_p, 0)
+
+    def attend(i, _):
+        for t in (2 * i, 2 * i + 1):
+            v_t = vb[t].reshape(128, KVW)
+            low = lax.dot_general(pt_r[t, 0:64], v_t[0:64], TN, preferred_element_type=F32).astype(BF16)
+            high = lax.dot_general(pt_r[t, 64:192], v_t, TN, preferred_element_type=F32).astype(BF16)
+            for half, part in ((0, low), (1, high)):
+                for s in range(GROUP):
+                    for g in range(KV_HEADS):
+                        lane = g * 1024 + s * 128
+                        att[t, half * 16:(half + 1) * 16, lane:lane + 128] = (
+                            part[s * 16:(s + 1) * 16, g * 128:(g + 1) * 128]
+                        )
+        return 0
+
+    lax.fori_loop(0, N_DP // 2, attend, 0)
 
     for d in (1, 2, 3):
         a2_copy(d).wait_recv()
     own_a = pl.ds(pl.multiple_of(y * 64, 16), 64)
+    own_cols = pl.ds(pl.multiple_of(x * 1024, 128), 1024)
     s3[0] = (
         a1[own_a].astype(F32) + a2_r[0].astype(F32) + a2_r[1].astype(F32) + a2_r[2].astype(F32)
     ).astype(BF16)
@@ -362,13 +494,12 @@
     for k in (4, 3, 5, 2, 6, 1, 7):
         z_copy(k).start()
 
-    v_copy.wait()
-    values = ((v_s[0:TOK] + v_r[...]) * inverse).astype(BF16)
-    values_pad = dot(st_ref[...], values).astype(BF16).reshape(N_DP, 2, 16, KVW)
-    vb[...] = jnp.zeros_like(vb)
-    for g in range(KV_HEADS):
-        lanes = slice(g * 128, (g + 1) * 128)
-        vb[:, :, g, :, lanes] = values_pad[:, :, :, lanes]
+    def place(i, _):
+        col = pl.ds(pl.multiple_of(i * 512, 128), 512)
+        out_ref[:, col] = dot(ft_ref[...], att[:, :, col].reshape(SLOTS, 512)).astype(BF16)
+        return 0
+
+    lax.fori_loop(0, QW // 512, place, 0)
 
     for k in range(1, 8):
         z_copy(k).wait_recv()
@@ -386,42 +517,12 @@
 
     lax.fori_loop(1, 16, start_f, 0)
 
-    def wait_p(i, _):
-        o = (p + i) % 16
-        remote(pt_s.at[o], pt_r.at[o], p_ss.at[o], p_rs.at[o], (o, f)).wait_recv()
-        return 0
-
-    lax.fori_loop(1, 16, wait_p, 0)
-
-    def attend(t, _):
-        v_t = vb[t].reshape(128, KVW)
-        low = lax.dot_general(pt_r[t, 0:64], v_t[0:64], TN, preferred_element_type=F32).astype(BF16)
-        high = lax.dot_general(pt_r[t, 64:192], v_t, TN, preferred_element_type=F32).astype(BF16)
-        for half, part in ((0, low), (1, high)):
-            for s in range(GROUP):
-                for g in range(KV_HEADS):
-                    lane = g * 1024 + s * 128
-                    att[t, half * 16:(half + 1) * 16, lane:lane + 128] = (
-                        part[s * 16:(s + 1) * 16, g * 128:(g + 1) * 128]
-                    )
-        return 0
-
-    lax.fori_loop(0, N_DP, attend, 0)
-
-    def place(i, _):
-        col = pl.ds(pl.multiple_of(i * 512, 128), 512)
-        out_ref[:, col] = lax.dot_general(
-            st_ref[...], att[:, :, col].reshape(SLOTS, 512), TN, preferred_element_type=F32
-        ).astype(BF16)
-        return 0
-
-    lax.fori_loop(0, QW // 512, place, 0)
-
     def wait_f(i, _):
         f_copy(i).wait_recv()
         return 0
 
     lax.fori_loop(1, 16, wait_f, 0)
+
     for core in range(2):
         for portion in range(2):
             pieces = []
@@ -431,12 +532,11 @@
             tall = jnp.concatenate(pieces, axis=0)
             grad_ref[core * DC:(core + 1) * DC, portion * 256:(portion + 1) * 256] = tall.T
 
+    for ring in (wx2[0], wx2[1], wy2, ring_a, ring_b):
+        ring.wait_send()
     for k in (1, 2, 3):
-        wx_copy(k).wait_send()
-        wx2_copy(k).wait_send()
-        wy2_copy(k).wait_send()
-        a_copy(k).wait_send()
-        b_copy(k).wait_send()
+        for j in range(CHUNKS):
+            wx_copy(j, k).wait_send()
         a2_copy(k).wait_send()
         b2_copy(k).wait_send()
     for k in range(1, 8):
@@ -471,8 +571,10 @@
         vmem((N_DP, CAP, KVW), BF16),
         vmem((2 * TOK, KVW), BF16),
         vmem((KVW, DH), BF16),
-        vmem((3, 256, 1024), BF16),
-        vmem((3, 64, DH), BF16),
+        vmem((2, 128, 1024), BF16),
+        vmem((2, 2, 128, 1024), BF16),
+        vmem((2, 32, DH), BF16),
+        vmem((2, 2, 32, DH), BF16),
         vmem((3, 64, 1024), BF16),
         vmem((3, 64, 1024), BF16),
         vmem((256, 1024), BF16),
@@ -485,13 +587,15 @@
         vmem((N_DP, 2, KV_HEADS, 16, KVW), BF16),
         vmem((N_DP, CAP, QW), BF16),
         vmem((SLOTS, TOK), BF16),
+        vmem((TOK, SLOTS), BF16),
+        vmem((KVW, 2 * TOK), BF16),
         dma((5,)),
         dma, dma,
-        dma((3,)), dma((3,)), dma((16,)), dma((16,)),
-        dma((3,)), dma((3,)), dma((3,)), dma((3,)),
+        dma((3 * CHUNKS,)), dma((3 * CHUNKS,)), dma((16,)), dma((16,)),
+        dma((6 * CHUNKS,)), dma((6 * CHUNKS,)), dma((6,)), dma((6,)),
         dma((16,)), dma((16,)), dma((16,)), dma((16,)),
         dma, dma, dma, dma,
-        dma((3,)), dma((3,)), dma((3,)), dma((3,)),
+        dma((6,)), dma((6,)), dma((6,)), dma((6,)),
         dma((3,)), dma((3,)), dma((3,)), dma((3,)),
         dma((7,)), dma((7,)), dma((15,)), dma((15,)),
     ]

time: 118 us -> 102 us (0.86)
  Pallas kernels: 111 us -> 95.5 us
    pallas_call x1, Pallas kernels: 111 us -> 95.5 us  [on_device(): pl.pallas_call(kernel, out_shape=(jax.ShapeDtypeStruct((TOK, QW), BF16),...]
where the time goes in v2:
time: 102 us
  Pallas kernels  95.5 us (94%)
  local copies, waits for them, and re-layouts  5.45 us (5%)
    pallas_call x1, Pallas kernels, on_device(): pl.pallas_call(kernel, out_shape=(jax.ShapeDtypeStruct((TOK, QW), BF16),...  95.5 us
    unnamed x4, local copies, waits for them, and re-layouts  4.19 us

profile of v2, /device:TPU:1, one launch (start us, length us, event | category | flops | bytes accessed | tf_op | source)
XLA Modules:
  0.0 101.6 jit_solution(13735320335122656407)
XLA Ops:
  0.6 1.3 %reshape.34.gain_ref = bf16[1,512]{1,0:T(2,128)(2,1)} reshape(bf16[512]{0:T(512)(128)(2,1)} %param.15) | data formatting | bytes 2048 | tf_op jit(solution)/shard_map/reshape | solution.py:625
  1.9 95.5 %value_path.1 = (bf16[256,4096]{1,0:T(8,128)(2,1)}, f32[512,512]{1,0:T(8,128)}) custom-call(bf16[256,8192]{1,0:T(8,128)(2,1)} %bitcast.8, s32[1,256]{1,0:T(1,128)} %bitcast.12, bf16[256,4096]{1,0:T(8,128)(2,1)} %bitcast.9, bf16[256,512]{1,0:T(8,128)(2,1)} %bitcast.11, bf16[256,4096]{1,0:T(8,128)(2,1)} %bitcast.10, s32[1,256]{1,0:T(1,128)} %bitcast.13, ...), custom_call_target="tpu_custom_call" | custom-call | flops 8000000000 | bytes 16777216 | tf_op jit(solution)/shard_map/value_path/pallas_call | solution.py:604
  97.4 0.0 copy-start
  97.5 3.2 %copy.12 = bf16[1,1,256,4096]{3,2,1,0:T(8,128)(2,1)} copy(bf16[1,1,256,4096]{3,2,1,0:T(8,128)(2,1)} %bitcast.7) | data formatting | bytes 4194304
  100.7 0.0 copy-done
  100.7 1.0 copy.13
Async XLA Ops:
  97.4 3.2 %copy-start = (f32[512,512]{1,0:T(8,128)S(1)}, f32[512,512]{1,0:T(8,128)}, u32[]{:S(2)}) copy-start(f32[512,512]{1,0:T(8,128)} %get-tuple-element.9) | copy-start | bytes 3145732

commit v3 on v2

--- a/solution.py
+++ b/solution.py
@@ -23,11 +23,15 @@
 DC = DSH // 2
 DH = D // 2
 EPS = 1e-05
-ROWS_X = 192
-CHUNKS = 2
-TRAIN = 3
+ROWS_X = 96
+CHUNKS = 1
+TRAIN = 8
+PARTS = 2
 ROWS_C = ROWS_X // CHUNKS
-ROWS_Y = (DC - ROWS_X) // 4
+ROWS_Y = 32
+ROWS_Z = DC - ROWS_X - ROWS_Y
+CHUNKS_Z = 2
+ROWS_ZC = ROWS_Z // CHUNKS_Z
 F32 = jnp.float32
 BF16 = jnp.bfloat16
 MESH = pl.DeviceIdType.MESH
@@ -95,16 +99,43 @@
             self.copy(i).wait_send()
 
 
+class PairRingGather:
+    def __init__(self, part, me, low, device, send, recv, base=0):
+        self.part, self.me, self.low, self.device = part, me, low, device
+        self.send, self.recv, self.base = send, recv, base
+
+    def copy(self, i):
+        out = 2 * self.low - 1
+        place, half, way = (
+            (0, None, out), (out, None, -out), (4 - out, 1 - self.low, out), (2, self.low, -out)
+        )[i]
+        part = self.part((self.me + place + 4) % 4, half)
+        return remote(
+            part, part, self.send.at[self.base + i], self.recv.at[self.base + i], self.device(way)
+        )
+
+    def step(self, i):
+        if i:
+            self.copy(i - 1).wait_recv()
+        if i < 4:
+            self.copy(i).start()
+
+    def wait_send(self):
+        for i in range(4):
+            self.copy(i).wait_send()
+
+
 class RingReduce:
-    def __init__(self, part, me, device, via, near, send, recv):
+    def __init__(self, part, me, device, via, near, send, recv, base=0):
         self.part, self.me, self.device = part, me, device
-        self.via, self.near, self.send, self.recv = via, near, send, recv
+        self.via, self.near, self.send, self.recv, self.base = via, near, send, recv, base
 
     def copy(self, i):
         place, half, way = ((2, 0, 1), (2, 1, -1), (1, 1, 1), (-1, 0, -1), (1, 0, 1), (-1, 1, -1))[i]
         to = self.via.at[half] if i < 2 else self.near.at[0 if way == 1 else 1, half]
         return remote(
-            self.part((self.me + place) % 4, half), to, self.send.at[i], self.recv.at[i], self.device(way)
+            self.part((self.me + place) % 4, half), to,
+            self.send.at[self.base + i], self.recv.at[self.base + i], self.device(way),
         )
 
     def forward(self):
@@ -131,11 +162,12 @@
     rows_ref, target_ref, q_ref, keys_ref, cot_ref, seg_ref, gain_ref, w_ref,
     out_ref, grad_ref,
     r_all, r_other, w_all, q_buf, c_buf, w_buf, qr, cr, kb, pt_s, pt_r, g_s, g_r, g_own,
-    gt, a_via, a_near, b_via, b_near, a2_r, b2_r, a1, b1, s3, r3, fin, v_s, v_r, vb, att, st_ref,
+    gt, a_via, a_near, b_via, b_near, a2_r, b2_r, a1, b1, s3, r3, fin, v_s, v_r, vb, out_buf, st_ref,
     ft_ref, gw,
     local_sem, row_s, row_r, wx_s, wx_r, wy_s, wy_r, wx2_s, wx2_r, wy2_s, wy2_r,
+    wz_s, wz_r, wz2_s, wz2_r,
     g_ss, g_rs, p_ss, p_rs, go_s, go_r, v_ss, v_rs,
-    a_ss, a_rs, b_ss, b_rs, a2_ss, a2_rs, b2_ss, b2_rs, z_ss, z_rs, f_ss, f_rs,
+    a_ss, a_rs, b_ss, b_rs, a2_ss, a2_rs, b2_ss, b2_rs, z_ss, z_rs, f_ss, f_rs, fs_s, fs_r, out_sem,
 ):
     p = lax.axis_index("dp")
     f = lax.axis_index("fsdp")
@@ -203,25 +235,64 @@
     lax.fori_loop(0, 12, greet_other, 0)
 
     loads[0].wait()
-    own_gain = gain_ref[:, pl.ds(pl.multiple_of(c * DC, 128), DC)]
+    own_gain = gain_ref[pl.ds(pl.multiple_of(c * DC, 128), DC)].reshape(1, DC)
     eye = lax.broadcasted_iota(jnp.int32, (DC, DC), 0) == lax.broadcasted_iota(jnp.int32, (DC, DC), 1)
     diagonal = jnp.where(eye, jnp.broadcast_to(own_gain.astype(F32), (DC, DC)), 0.0).astype(BF16)
-    w_all[f] = dot(diagonal, w_buf[...]).astype(BF16)
+    w_all[x, zh] = dot(diagonal, w_buf[...]).astype(BF16)
     onehot = slot_matrix(seg_ref[...])
     pl.semaphore_wait(barrier, 30 + 12)
 
-    y_rows = pl.ds(pl.multiple_of(ROWS_X + y * ROWS_Y, 16), ROWS_Y)
+    y_cols = pl.ds(pl.multiple_of(y * (KVW // 4), 128), KVW // 4)
 
     def wx_copy(j, k):
-        part = w_all.at[f, pl.ds(j * ROWS_C, ROWS_C)]
+        part = w_all.at[x, zh, pl.ds(j * ROWS_C, ROWS_C)]
         i = j * 3 + k - 1
         return remote(part, part, wx_s.at[i], wx_r.at[i], at_z(z + sgn * k, y, x))
 
     def wy_copy(i):
-        part = w_all.at[f, y_rows]
+        part = w_all.at[x, zh, pl.ds(ROWS_X, ROWS_Y), y_cols]
         return remote(part, part, wy_s.at[i], wy_r.at[i], at_z(z + sgn * (i % 4), y, (x + i // 4) % 4))
 
-    for j in range(CHUNKS):
+    def x_part(j):
+        def part(xx, half):
+            return w_all.at[xx, :, pl.ds(j * ROWS_C + half * (ROWS_C // 2), ROWS_C // 2)]
+
+        return part
+
+    wx2 = [RingGather(x_part(j), x, at_x, wx2_s, wx2_r, 6 * j) for j in range(CHUNKS)]
+
+    def y_part(yy, half):
+        cols = pl.ds(pl.multiple_of(yy * (KVW // 4), 128), KVW // 4)
+        return w_all.at[pl.ds(half * 2, 2), :, pl.ds(ROWS_X, ROWS_Y), cols]
+
+    wy2 = RingGather(y_part, y, at_y, wy2_s, wy2_r)
+
+    first_z, rows_z = DC - ROWS_Z, ROWS_Z // 2
+
+    def zx_part(xx, half):
+        return w_all.at[xx, zh, pl.ds(first_z + half * rows_z, rows_z)]
+
+    def z_ring_part(j):
+        def part(zz, half):
+            first = first_z + j * ROWS_ZC
+            if half is None:
+                return w_all.at[:, zz, pl.ds(first, ROWS_ZC)]
+            first = first + half * (ROWS_ZC // 2)
+            return w_all.at[:, zz, pl.ds(pl.multiple_of(first, 16), ROWS_ZC // 2)]
+
+        return part
+
+    wz = RingGather(zx_part, x, at_x, wz_s, wz_r)
+    wz2 = [
+        PairRingGather(z_ring_part(j), zh, zl, lambda way: at_z(z + way, y, x), wz2_s, wz2_r, 4 * j)
+        for j in range(CHUNKS_Z)
+    ]
+
+    def step_wz2(i):
+        for ring in wz2:
+            ring.step(i)
+
+    def start_wx(j):
         for k in (3, 2, 1):
             wx_copy(j, k).start()
 
@@ -229,7 +300,8 @@
         wy_copy(i).start()
         return 0
 
-    lax.fori_loop(1, 16, start_wy, 0)
+    wz.start()
+    start_wx(0)
 
     row_copy = remote(r_other, r_all.at[pl.ds(TOK, TOK)], row_s, row_r, sibling)
     pltpu.make_async_copy(r_other, r_other, local_sem.at[3]).wait()
@@ -251,6 +323,9 @@
             part = slice(s * 128, (s + 1) * 128)
             qr[:, :, s, :, lanes] = q_pad[:, :, :, part]
             cr[:, :, s, :, lanes] = c_pad[:, :, :, part]
+
+    wz.forward()
+    lax.fori_loop(1, 16, start_wy, 0)
 
     row_i = lax.broadcasted_iota(jnp.int32, (128, 256), 0)
     col_i = lax.broadcasted_iota(jnp.int32, (128, 256), 1)
@@ -288,48 +363,31 @@
             pt_s[o, 0:64] = prob[0:64, 0:128]
             pt_s[o, 64:192] = prob[:, 128:256]
 
-    def x_part(j):
-        def part(xx, half):
-            return w_all.at[pl.ds(xx * 4, 4), pl.ds(j * ROWS_C + half * (ROWS_C // 2), ROWS_C // 2)]
-
-        return part
-
-    wx2 = [RingGather(x_part(j), x, at_x, wx2_s, wx2_r, 6 * j) for j in range(CHUNKS)]
-
-    def y_part(yy, half):
-        rows = pl.ds(pl.multiple_of(ROWS_X + yy * ROWS_Y, 16), ROWS_Y)
-        return w_all.at[pl.ds(half * 8, 8), rows]
-
-    wy2 = RingGather(y_part, y, at_y, wy2_s, wy2_r)
-
     def trainer_step(i, _):
         owners = [(p + 1 + i * TRAIN + j) % 16 for j in range(TRAIN)]
         trainer(owners)
-        for o in owners:
+        for o in owners[:-1]:
             g_copy(o).start()
 
-        @pl.when(i == 1)
+        @pl.when(i == 0)
         def _():
-            for k in (1, 2, 3):
-                wx_copy(0, k).wait_recv()
-            wx2[0].start()
-
-        return 0
-
-    lax.fori_loop(0, 15 // TRAIN, trainer_step, 0)
-    trainer([p])
+            g_copy(owners[-1]).start()
+
+        return 0
+
+    lax.fori_loop(0, 16 // TRAIN, trainer_step, 0)
+
     g_r[p] = g_s[p]
     pt_r[p] = pt_s[p]
 
-    def start_p(i, _):
-        p_copy((p + i) % 16).start()
-        return 0
-
-    lax.fori_loop(1, 16, start_p, 0)
-    for k in (1, 2, 3):
-        wx_copy(1, k).wait_recv()
-    wx2[0].forward()
-    wx2[1].start()
+    def wait_wx(j):
+        for k in (1, 2, 3):
+            wx_copy(j, k).wait_recv()
+
+    wz.finish()
+    step_wz2(0)
+    wait_wx(0)
+    wx2[0].start()
 
     pltpu.make_async_copy(r_other, r_other, local_sem.at[4]).wait()
 
@@ -346,17 +404,25 @@
     st_ref[...] = owner_hot
     ft_ref[...] = owner_tall
 
+    def start_p(i, _):
+        p_copy((p + i) % 16).start()
+        return 0
+
+    lax.fori_loop(1, 16, start_p, 0)
+
     def wait_g(i, _):
         o = (p + i) % 16
         remote(g_s.at[o], g_r.at[o], g_ss.at[o], g_rs.at[o], (o, f)).wait_recv()
         return 0
 
     lax.fori_loop(1, 16, wait_g, 0)
+
     owner_grad = dot(owner_tall, g_r[...].reshape(SLOTS, KVW))
     g_own[0:TOK] = (owner_grad * inverse).astype(BF16)
     go_copy = remote(g_own.at[pl.ds(0, TOK)], g_own.at[pl.ds(TOK, TOK)], go_s, go_r, sibling)
     go_copy.start()
-    row_copy.wait()
+
+    wx2[0].forward()
 
     def wait_wy(i, _):
         wy_copy(i).wait_recv()
@@ -364,79 +430,141 @@
 
     lax.fori_loop(1, 16, wait_wy, 0)
     wy2.start()
+
+    row_copy.wait()
     go_copy.wait()
 
-    def a_part(xx, half):
-        return gt.at[pl.ds(half * 128, 128), pl.ds(pl.multiple_of(xx * 1024, 128), 1024)]
-
-    def b_part(yy, half):
-        return gt.at[pl.ds(pl.multiple_of(256 + yy * 64 + half * 32, 16), 32)]
-
-    ring_a = RingReduce(a_part, x, at_x, a_via, a_near, a_ss, a_rs)
-    ring_b = RingReduce(b_part, y, at_y, b_via, b_near, b_ss, b_rs)
+    def a_part(q):
+        def part(xx, half):
+            return gt.at[
+                pl.ds(q * 128 + half * 64, 64), pl.ds(pl.multiple_of(xx * 1024, 128), 1024)
+            ]
+
+        return part
+
+    def b_part(q):
+        def part(yy, half):
+            return gt.at[pl.ds(pl.multiple_of(256 + yy * 64 + q * 32 + half * 16, 16), 16)]
+
+        return part
+
+    ring_a = [
+        RingReduce(a_part(q), x, at_x, a_via.at[q], a_near.at[q], a_ss, a_rs, 6 * q) for q in range(PARTS)
+    ]
+    ring_b = [
+        RingReduce(b_part(q), y, at_y, b_via.at[q], b_near.at[q], b_ss, b_rs, 6 * q) for q in range(PARTS)
+    ]
     gw[...] = g_own[...].T
 
-    def partial(portion):
-        def step(i, base):
-            col = pl.ds(pl.multiple_of(base + i * 512, 128), 512)
-            rows = slice(portion * 256, (portion + 1) * 256)
-            gt[rows, col] = dot(gw[rows], r_all[:, col]).astype(BF16)
-            return base
-
-        return step
-
-    def partial_a(d):
-        lax.fori_loop(0, 2, partial(0), ((x + d) % 4) * 1024)
-
-    partial_a(2)
-    ring_a.copy(0).start()
-    ring_a.copy(1).start()
-    lax.fori_loop(0, 8, partial(1), 0)
-    for i in (0, 1, 2, 3):
-        ring_b.copy(i).start()
-    partial_a(1)
-    ring_a.copy(2).start()
-    partial_a(3)
-    ring_a.copy(3).start()
-    partial_a(0)
-
-    wx2[1].forward()
+    def partial(d):
+        col = pl.ds(pl.multiple_of(((x + d) % 4) * 1024, 128), 1024)
+        gt[:, col] = dot(gw[...], r_all[:, col]).astype(BF16)
+
+    partial(2)
+    ring_a[0].copy(0).start()
+    ring_a[0].copy(1).start()
+    partial(1)
+    ring_a[0].copy(2).start()
+    partial(3)
+    ring_a[0].copy(3).start()
+    partial(0)
+    for i in range(4):
+        ring_b[0].copy(i).start()
+    for i in range(4):
+        ring_a[1].copy(i).start()
+    for i in range(4):
+        ring_b[1].copy(i).start()
+
+    step_wz2(1)
+
+    ring_a[0].forward()
+
+    ring_b[0].forward()
+
+    step_wz2(2)
+
+    ring_a[1].forward()
+
+    ring_b[1].forward()
+
     wy2.forward()
 
-    ring_a.forward()
-    ring_b.forward()
-
-    for ring in (wx2[0], wx2[1], wy2):
+    def a2_copy(q, d):
+        part = a1.at[q, pl.ds(pl.multiple_of(((y + d) % 4) * 32, 16), 32)]
+        i = q * 3 + d - 1
+        return remote(part, a2_r.at[q, d - 1], a2_ss.at[i], a2_rs.at[i], at_y(d))
+
+    def b2_copy(q, d):
+        part = b1.at[q, :, pl.ds(pl.multiple_of(((x + d) % 4) * 1024, 128), 1024)]
+        i = q * 3 + d - 1
+        return remote(part, b2_r.at[q, d - 1], b2_ss.at[i], b2_rs.at[i], at_x(d))
+
+    def second_a(q):
+        ring_a[q].finish()
+        for half in range(2):
+            a1[q, half * 64:(half + 1) * 64] = ring_a[q].total(half).astype(BF16)
+        for d in (2, 1, 3):
+            a2_copy(q, d).start()
+
+    def second_b(q):
+        ring_b[q].finish()
+        for half in range(2):
+            b1[q, half * 16:(half + 1) * 16] = ring_b[q].total(half).astype(BF16)
+        for d in (2, 1, 3):
+            b2_copy(q, d).start()
+
+    second_a(0)
+    second_b(0)
+
+    step_wz2(3)
+
+    second_a(1)
+
+    second_b(1)
+
+    for ring in wx2 + [wy2]:
         ring.finish()
-    for m in (1, 0):
-        for n in range(2):
-            cols = slice(n * 256, (n + 1) * 256)
-            rows = slice(m * TOK, (m + 1) * TOK)
-            v_s[rows, cols] = dot(r_all[rows], w_all[:, :, cols].reshape(DH, 256))
-        if m == 1:
-            v_copy = remote(v_s.at[pl.ds(TOK, TOK)], v_r, v_ss, v_rs, sibling)
-            v_copy.start()
-
-    ring_a.finish()
-    for half in range(2):
-        a1[half * 128:(half + 1) * 128] = ring_a.total(half).astype(BF16)
-
-    def a2_copy(d):
-        part = a1.at[pl.ds(pl.multiple_of(((y + d) % 4) * 64, 16), 64)]
-        return remote(part, a2_r.at[d - 1], a2_ss.at[d - 1], a2_rs.at[d - 1], at_y(d))
-
-    for d in (2, 1, 3):
-        a2_copy(d).start()
-    ring_b.finish()
-    for half in range(2):
-        b1[half * 32:(half + 1) * 32] = ring_b.total(half).astype(BF16)
-
-    def b2_copy(d):
-        part = b1.at[:, pl.ds(pl.multiple_of(((x + d) % 4) * 1024, 128), 1024)]
-        return remote(part, b2_r.at[d - 1], b2_ss.at[d - 1], b2_rs.at[d - 1], at_x(d))
-
-    for d in (2, 1, 3):
-        b2_copy(d).start()
+    step_wz2(4)
+
+    for n in range(2):
+        cols = slice(n * 256, (n + 1) * 256)
+        v_s[:, cols] = dot(r_all[...], w_all[:, :, :, cols].reshape(DH, 256))
+    v_copy = remote(v_s.at[pl.ds(TOK, TOK)], v_r, v_ss, v_rs, sibling)
+    v_copy.start()
+
+    own_a = pl.ds(pl.multiple_of(y * 32, 16), 32)
+    own_cols = pl.ds(pl.multiple_of(x * 1024, 128), 1024)
+
+    def z_part(q, zz):
+        zz = lax.rem(zz, 8)
+        return s3.at[
+            q, :, pl.ds(pl.multiple_of((zz % 2) * 16, 16), 16),
+            pl.ds(pl.multiple_of((zz // 2) * DC, 128), DC),
+        ]
+
+    def z_copy(q, k):
+        i = q * 7 + k - 1
+        return remote(z_part(q, z + k), r3.at[q, k - 1], z_ss.at[i], z_rs.at[i], at_z(z + k, y, x))
+
+    def third(q):
+        for d in (1, 2, 3):
+            a2_copy(q, d).wait_recv()
+        total = a1[q, own_a].astype(F32)
+        for d in range(3):
+            total = total + a2_r[q, d].astype(F32)
+        s3[q, 0] = total.astype(BF16)
+        for d in (1, 2, 3):
+            b2_copy(q, d).wait_recv()
+        total = b1[q, :, own_cols].astype(F32)
+        for d in range(3):
+            total = total + b2_r[q, d].astype(F32)
+        s3[q, 1] = total.astype(BF16)
+        for k in (4, 3, 5, 2, 6, 1, 7):
+            z_copy(q, k).start()
+
+    third(0)
+
+    third(1)
 
     v_copy.wait()
     values = ((v_s[0:TOK] + v_r[...]) * inverse).astype(BF16)
@@ -454,99 +582,92 @@
     lax.fori_loop(1, 16, wait_p, 0)
 
     def attend(i, _):
-        for t in (2 * i, 2 * i + 1):
+        for t in range(4):
+            t = 4 * i + t
             v_t = vb[t].reshape(128, KVW)
             low = lax.dot_general(pt_r[t, 0:64], v_t[0:64], TN, preferred_element_type=F32).astype(BF16)
             high = lax.dot_general(pt_r[t, 64:192], v_t, TN, preferred_element_type=F32).astype(BF16)
-            for half, part in ((0, low), (1, high)):
-                for s in range(GROUP):
-                    for g in range(KV_HEADS):
-                        lane = g * 1024 + s * 128
-                        att[t, half * 16:(half + 1) * 16, lane:lane + 128] = (
-                            part[s * 16:(s + 1) * 16, g * 128:(g + 1) * 128]
-                        )
-        return 0
-
-    lax.fori_loop(0, N_DP // 2, attend, 0)
-
-    for d in (1, 2, 3):
-        a2_copy(d).wait_recv()
-    own_a = pl.ds(pl.multiple_of(y * 64, 16), 64)
-    own_cols = pl.ds(pl.multiple_of(x * 1024, 128), 1024)
-    s3[0] = (
-        a1[own_a].astype(F32) + a2_r[0].astype(F32) + a2_r[1].astype(F32) + a2_r[2].astype(F32)
-    ).astype(BF16)
-    for d in (1, 2, 3):
-        b2_copy(d).wait_recv()
-    s3[1] = (
-        b1[:, own_cols].astype(F32) + b2_r[0].astype(F32) + b2_r[1].astype(F32) + b2_r[2].astype(F32)
-    ).astype(BF16)
-
-    def z_part(zz):
-        zz = lax.rem(zz, 8)
-        return s3.at[
-            :, pl.ds(pl.multiple_of((zz % 2) * 32, 16), 32), pl.ds(pl.multiple_of((zz // 2) * DC, 128), DC)
-        ]
-
-    def z_copy(k):
-        return remote(z_part(z + k), r3.at[k - 1], z_ss.at[k - 1], z_rs.at[k - 1], at_z(z + k, y, x))
-
-    for k in (4, 3, 5, 2, 6, 1, 7):
-        z_copy(k).start()
-
-    def place(i, _):
-        col = pl.ds(pl.multiple_of(i * 512, 128), 512)
-        out_ref[:, col] = dot(ft_ref[...], att[:, :, col].reshape(SLOTS, 512)).astype(BF16)
-        return 0
-
-    lax.fori_loop(0, QW // 512, place, 0)
-
-    for k in range(1, 8):
-        z_copy(k).wait_recv()
-    total = z_part(z)[...].astype(F32)
-    for k in range(7):
-        total = total + r3[k].astype(F32)
-    fin[p] = (total * own_gain.astype(F32).reshape(1, 1, DC)).astype(BF16)
-
-    def f_copy(i):
-        return remote(fin.at[p], fin.at[p], f_ss.at[i - 1], f_rs.at[i - 1], ((p + i) % 16, f))
-
-    def start_f(i, _):
-        f_copy(i).start()
-        return 0
-
-    lax.fori_loop(1, 16, start_f, 0)
-
-    def wait_f(i, _):
-        f_copy(i).wait_recv()
-        return 0
-
-    lax.fori_loop(1, 16, wait_f, 0)
+            qr[t, 0] = low.reshape(GROUP, 16, KVW)
+            qr[t, 1] = high.reshape(GROUP, 16, KVW)
+        return 0
+
+    lax.fori_loop(0, N_DP // 4, attend, 0)
+
+    def f_copy(q, i):
+        j = q * 7 + i - 1
+        part = fin.at[q, c, p // 2]
+        return remote(part, part, f_ss.at[j], f_rs.at[j], ((p // 2 + i) % 8 * 2 + c, f))
+
+    def fs_copy(q):
+        part = fin.at[q, c]
+        return remote(part, part, fs_s.at[q], fs_r.at[q], sibling)
+
+    def last(q):
+        for k in range(1, 8):
+            z_copy(q, k).wait_recv()
+        total = z_part(q, z)[...].astype(F32)
+        for k in range(7):
+            total = total + r3[q, k].astype(F32)
+        fin[q, c, p // 2] = (total * own_gain.astype(F32).reshape(1, 1, DC)).astype(BF16)
+
+        def start_f(i, _):
+            f_copy(q, i).start()
+            return 0
+
+        lax.fori_loop(1, 8, start_f, 0)
+
+    last(0)
+
+    last(1)
+
+    out_copies = []
+    for g in range(KV_HEADS):
+        lanes = slice(g * 128, (g + 1) * 128)
+        wide = slice(g * 1024, (g + 1) * 1024)
+        heads = [qr[:, :, s, :, lanes].reshape(SLOTS, 128) for s in range(GROUP)]
+        out_buf[:, wide] = dot(ft_ref[...], jnp.concatenate(heads, axis=1)).astype(BF16)
+        out_copies.append(
+            pltpu.make_async_copy(out_buf.at[:, wide], out_ref.at[:, wide], out_sem.at[g])
+        )
+        out_copies[-1].start()
+
+    for q in range(PARTS):
+        for i in range(1, 8):
+            f_copy(q, i).wait_recv()
+        fs_copy(q).start()
+    for q in range(PARTS):
+        fs_copy(q).wait_recv()
 
     for core in range(2):
         for portion in range(2):
             pieces = []
-            for yy in range(4):
-                for zz in range(2):
-                    pieces.append(fin[(zz * 4 + yy) * 2 + core, portion].astype(F32))
+            for i in range(16):
+                yy, q, zz = (i // 2 % 4, i // 8, i % 2) if portion == 0 else (i // 4, i // 2 % 2, i % 2)
+                pieces.append(fin[q, core, zz * 4 + yy, portion].astype(F32))
             tall = jnp.concatenate(pieces, axis=0)
             grad_ref[core * DC:(core + 1) * DC, portion * 256:(portion + 1) * 256] = tall.T
 
-    for ring in (wx2[0], wx2[1], wy2, ring_a, ring_b):
+    for cp in out_copies:
+        cp.wait()
+    for ring in wx2 + [wy2, wz] + wz2 + ring_a + ring_b:
         ring.wait_send()
     for k in (1, 2, 3):
         for j in range(CHUNKS):
             wx_copy(j, k).wait_send()
-        a2_copy(k).wait_send()
-        b2_copy(k).wait_send()
+        for q in range(PARTS):
+            a2_copy(q, k).wait_send()
+            b2_copy(q, k).wait_send()
     for k in range(1, 8):
-        z_copy(k).wait_send()
+        for q in range(PARTS):
+            z_copy(q, k).wait_send()
+            f_copy(q, k).wait_send()
+    for q in range(PARTS):
+        fs_copy(q).wait_send()
 
     def wait_sends(i, _):
         wy_copy(i).wait_send()
         g_copy((p + i) % 16).wait_send()
         p_copy((p + i) % 16).wait_send()
-        f_copy(i).wait_send()
         return 0
 
     lax.fori_loop(1, 16, wait_sends, 0)
@@ -558,7 +679,7 @@
     scratch = [
         vmem((2 * TOK, DH), BF16),
         vmem((TOK, DH), BF16),
-        vmem((N_FSDP, DC, KVW), BF16),
+        vmem((4, 4, DC, KVW), BF16),
         vmem((TOK, QW), BF16),
         vmem((TOK, QW), BF16),
         vmem((DC, KVW), BF16),
@@ -571,21 +692,21 @@
         vmem((N_DP, CAP, KVW), BF16),
         vmem((2 * TOK, KVW), BF16),
         vmem((KVW, DH), BF16),
-        vmem((2, 128, 1024), BF16),
-        vmem((2, 2, 128, 1024), BF16),
-        vmem((2, 32, DH), BF16),
-        vmem((2, 2, 32, DH), BF16),
-        vmem((3, 64, 1024), BF16),
-        vmem((3, 64, 1024), BF16),
-        vmem((256, 1024), BF16),
-        vmem((64, DH), BF16),
-        vmem((2, 64, 1024), BF16),
-        vmem((7, 2, 32, DC), BF16),
-        vmem((N_DP, 2, 32, DC), BF16),
+        vmem((PARTS, 2, 64, 1024), BF16),
+        vmem((PARTS, 2, 2, 64, 1024), BF16),
+        vmem((PARTS, 2, 16, DH), BF16),
+        vmem((PARTS, 2, 2, 16, DH), BF16),
+        vmem((PARTS, 3, 32, 1024), BF16),
+        vmem((PARTS, 3, 32, 1024), BF16),
+        vmem((PARTS, 128, 1024), BF16),
+        vmem((PARTS, 32, DH), BF16),
+        vmem((PARTS, 2, 32, 1024), BF16),
+        vmem((PARTS, 7, 2, 16, DC), BF16),
+        vmem((PARTS, 2, 8, 2, 16, DC), BF16),
         vmem((2 * TOK, KVW), F32),
         vmem((TOK, KVW), F32),
         vmem((N_DP, 2, KV_HEADS, 16, KVW), BF16),
-        vmem((N_DP, CAP, QW), BF16),
+        vmem((TOK, QW), BF16),
         vmem((SLOTS, TOK), BF16),
         vmem((TOK, SLOTS), BF16),
         vmem((KVW, 2 * TOK), BF16),
@@ -593,11 +714,13 @@
         dma, dma,
         dma((3 * CHUNKS,)), dma((3 * CHUNKS,)), dma((16,)), dma((16,)),
         dma((6 * CHUNKS,)), dma((6 * CHUNKS,)), dma((6,)), dma((6,)),
+        dma((6,)), dma((6,)), dma((4 * CHUNKS_Z,)), dma((4 * CHUNKS_Z,)),
         dma((16,)), dma((16,)), dma((16,)), dma((16,)),
         dma, dma, dma, dma,
+        dma((12,)), dma((12,)), dma((12,)), dma((12,)),
         dma((6,)), dma((6,)), dma((6,)), dma((6,)),
-        dma((3,)), dma((3,)), dma((3,)), dma((3,)),
-        dma((7,)), dma((7,)), dma((15,)), dma((15,)),
+        dma((14,)), dma((14,)), dma((14,)), dma((14,)), dma((2,)), dma((2,)),
+        dma((KV_HEADS,)),
     ]
     anywhere = pl.BlockSpec(memory_space=pl.ANY)
     inside = pl.BlockSpec(memory_space=pltpu.VMEM)
@@ -608,7 +731,7 @@
             jax.ShapeDtypeStruct((DSH, KVW), F32),
         ),
         in_specs=[anywhere, inside, anywhere, inside, anywhere, inside, inside, anywhere],
-        out_specs=(inside, inside),
+        out_specs=(anywhere, inside),
         scratch_shapes=scratch,
         compiler_params=pltpu.CompilerParams(
             collective_id=0, has_side_effects=True, vmem_limit_bytes=60 * 2**20
@@ -622,7 +745,7 @@
         keys.reshape(TOK, KVW),
         cotangent.reshape(TOK, QW),
         segment.reshape(1, TOK),
-        norm_gain.reshape(1, DSH),
+        norm_gain,
         value_weight,
     )
     return (returned.reshape(1, 1, TOK, QW), gradient)

time: 102 us -> 84.2 us (0.83)
  Pallas kernels: 95.5 us -> 79.3 us
  local copies, waits for them, and re-layouts: 5.45 us -> 4.19 us
    pallas_call x1, Pallas kernels: 95.5 us -> 79.3 us  [on_device(): pl.pallas_call(kernel, out_shape=(jax.ShapeDtypeStruct((TOK, QW), BF16),...]
    reshape x1 -> x0, local copies, waits for them, and re-layouts: 1.26 us -> none  [on_device(): norm_gain.reshape(1, DSH)]
where the time goes in v3:
time: 84.2 us; the launch traced here: 84.1 us
  Pallas kernels  79.3 us (94%)
  local copies, waits for them, and re-layouts  4.19 us (5%)
    pallas_call x1, Pallas kernels, on_device(): pl.pallas_call(kernel, out_shape=(jax.ShapeDtypeStruct((TOK, QW), BF16),...  79.3 us
    unnamed x4, local copies, waits for them, and re-layouts  4.19 us

profile of v3, /device:TPU:1, one launch (start us, length us, event | category | flops | bytes accessed | tf_op | source)
XLA Modules:
  0.0 84.1 jit_solution(13871035647980396705)
XLA Ops:
  0.6 79.3 %value_path.1 = (bf16[256,4096]{1,0:T(8,128)(2,1)}, f32[512,512]{1,0:T(8,128)}) custom-call(bf16[256,8192]{1,0:T(8,128)(2,1)} %bitcast.8, s32[1,256]{1,0:T(1,128)} %bitcast.12, bf16[256,4096]{1,0:T(8,128)(2,1)} %bitcast.9, bf16[256,512]{1,0:T(8,128)(2,1)} %bitcast.11, bf16[256,4096]{1,0:T(8,128)(2,1)} %bitcast.10, s32[1,256]{1,0:T(1,128)} %bitcast.13, ...), custom_call_target="tpu_custom_call" | custom-call | flops 8000000000 | bytes 16777216 | tf_op jit(solution)/shard_map/value_path/pallas_call | solution.py:727
  79.9 0.0 copy-start
  79.9 3.2 %copy.12 = bf16[1,1,256,4096]{3,2,1,0:T(8,128)(2,1)} copy(bf16[1,1,256,4096]{3,2,1,0:T(8,128)(2,1)} %bitcast.7) | data formatting | bytes 4194304
  83.1 0.0 copy-done
  83.1 1.0 %copy.13 = f32[512,512]{1,0:T(8,128)} copy(f32[512,512]{1,0:T(8,128)S(1)} %copy-done) | data formatting | bytes 2097152
Async XLA Ops:
  79.9 3.2 %copy-start = (f32[512,512]{1,0:T(8,128)S(1)}, f32[512,512]{1,0:T(8,128)}, u32[]{:S(2)}) copy-start(f32[512,512]{1,0:T(8,128)} %get-tuple-element.9) | copy-start | bytes 3145732

commit v4 on v3

--- a/solution.py
+++ b/solution.py
@@ -24,14 +24,15 @@
 DH = D // 2
 EPS = 1e-05
 ROWS_X = 96
-CHUNKS = 1
+CHUNKS = ((0, 32), (32, 64))
+ROWS_Z = DC - ROWS_X
+CHUNKS_Z = ((0, 64), (64, 96))
+FIRST_X = ROWS_Z
 TRAIN = 8
 PARTS = 2
-ROWS_C = ROWS_X // CHUNKS
-ROWS_Y = 32
-ROWS_Z = DC - ROWS_X - ROWS_Y
-CHUNKS_Z = 2
-ROWS_ZC = ROWS_Z // CHUNKS_Z
+PART_A = 256 // PARTS
+PART_B = 64 // PARTS
+HALF = DC // 2
 F32 = jnp.float32
 BF16 = jnp.bfloat16
 MESH = pl.DeviceIdType.MESH
@@ -164,7 +165,7 @@
     r_all, r_other, w_all, q_buf, c_buf, w_buf, qr, cr, kb, pt_s, pt_r, g_s, g_r, g_own,
     gt, a_via, a_near, b_via, b_near, a2_r, b2_r, a1, b1, s3, r3, fin, v_s, v_r, vb, out_buf, st_ref,
     ft_ref, gw,
-    local_sem, row_s, row_r, wx_s, wx_r, wy_s, wy_r, wx2_s, wx2_r, wy2_s, wy2_r,
+    local_sem, row_s, row_r, wx_s, wx_r, wx2_s, wx2_r,
     wz_s, wz_r, wz2_s, wz2_r,
     g_ss, g_rs, p_ss, p_rs, go_s, go_r, v_ss, v_rs,
     a_ss, a_rs, b_ss, b_rs, a2_ss, a2_rs, b2_ss, b2_rs, z_ss, z_rs, f_ss, f_rs, fs_s, fs_r, out_sem,
@@ -218,21 +219,19 @@
 
     def greet(i, _):
         pl.semaphore_signal(barrier, inc=1, device_id=((p + i) % 16, f), device_id_type=MESH)
-        pl.semaphore_signal(barrier, inc=1, device_id=(p, (f + i) % 16), device_id_type=MESH)
         return 0
 
     lax.fori_loop(1, 16, greet, 0)
 
-    def greet_other(i, _):
-        dx, dz = i // 3, 1 + i % 3
-        pl.semaphore_signal(
-            barrier, inc=1,
-            device_id=(((1 - zl) * 4 + y) * 2 + c, ((x + dx) % 4) * 4 + (zh + dz) % 4),
-            device_id_type=MESH,
-        )
-        return 0
-
-    lax.fori_loop(0, 12, greet_other, 0)
+    def greet_rings(i, _):
+        pl.semaphore_signal(barrier, inc=1, device_id=at_x(i), device_id_type=MESH)
+        beside = x * 4 + (zh + i) % 4
+        pl.semaphore_signal(barrier, inc=1, device_id=(p, beside), device_id_type=MESH)
+        other = ((1 - zl) * 4 + y) * 2 + c
+        pl.semaphore_signal(barrier, inc=1, device_id=(other, beside), device_id_type=MESH)
+        return 0
+
+    lax.fori_loop(1, 4, greet_rings, 0)
 
     loads[0].wait()
     own_gain = gain_ref[pl.ds(pl.multiple_of(c * DC, 128), DC)].reshape(1, DC)
@@ -240,68 +239,56 @@
     diagonal = jnp.where(eye, jnp.broadcast_to(own_gain.astype(F32), (DC, DC)), 0.0).astype(BF16)
     w_all[x, zh] = dot(diagonal, w_buf[...]).astype(BF16)
     onehot = slot_matrix(seg_ref[...])
-    pl.semaphore_wait(barrier, 30 + 12)
-
-    y_cols = pl.ds(pl.multiple_of(y * (KVW // 4), 128), KVW // 4)
+    pl.semaphore_wait(barrier, 15 + 9)
 
     def wx_copy(j, k):
-        part = w_all.at[x, zh, pl.ds(j * ROWS_C, ROWS_C)]
+        first, rows = CHUNKS[j]
+        part = w_all.at[x, zh, pl.ds(FIRST_X + first, rows)]
         i = j * 3 + k - 1
         return remote(part, part, wx_s.at[i], wx_r.at[i], at_z(z + sgn * k, y, x))
 
-    def wy_copy(i):
-        part = w_all.at[x, zh, pl.ds(ROWS_X, ROWS_Y), y_cols]
-        return remote(part, part, wy_s.at[i], wy_r.at[i], at_z(z + sgn * (i % 4), y, (x + i // 4) % 4))
-
     def x_part(j):
+        first, rows = CHUNKS[j]
+
         def part(xx, half):
-            return w_all.at[xx, :, pl.ds(j * ROWS_C + half * (ROWS_C // 2), ROWS_C // 2)]
+            return w_all.at[xx, :, pl.ds(FIRST_X + first + half * (rows // 2), rows // 2)]
 
         return part
 
-    wx2 = [RingGather(x_part(j), x, at_x, wx2_s, wx2_r, 6 * j) for j in range(CHUNKS)]
-
-    def y_part(yy, half):
-        cols = pl.ds(pl.multiple_of(yy * (KVW // 4), 128), KVW // 4)
-        return w_all.at[pl.ds(half * 2, 2), :, pl.ds(ROWS_X, ROWS_Y), cols]
-
-    wy2 = RingGather(y_part, y, at_y, wy2_s, wy2_r)
-
-    first_z, rows_z = DC - ROWS_Z, ROWS_Z // 2
+    wx2 = [RingGather(x_part(j), x, at_x, wx2_s, wx2_r, 6 * j) for j in range(len(CHUNKS))]
+
+    rows_z = ROWS_Z // 2
 
     def zx_part(xx, half):
-        return w_all.at[xx, zh, pl.ds(first_z + half * rows_z, rows_z)]
+        return w_all.at[xx, zh, pl.ds(half * rows_z, rows_z)]
 
     def z_ring_part(j):
         def part(zz, half):
-            first = first_z + j * ROWS_ZC
+            first, rows = CHUNKS_Z[j]
             if half is None:
-                return w_all.at[:, zz, pl.ds(first, ROWS_ZC)]
-            first = first + half * (ROWS_ZC // 2)
-            return w_all.at[:, zz, pl.ds(pl.multiple_of(first, 16), ROWS_ZC // 2)]
+                return w_all.at[:, zz, pl.ds(first, rows)]
+            first = first + half * (rows // 2)
+            return w_all.at[:, zz, pl.ds(pl.multiple_of(first, 16), rows // 2)]
 
         return part
 
     wz = RingGather(zx_part, x, at_x, wz_s, wz_r)
     wz2 = [
         PairRingGather(z_ring_part(j), zh, zl, lambda way: at_z(z + way, y, x), wz2_s, wz2_r, 4 * j)
-        for j in range(CHUNKS_Z)
+        for j in range(len(CHUNKS_Z))
     ]
-
-    def step_wz2(i):
-        for ring in wz2:
-            ring.step(i)
 
     def start_wx(j):
         for k in (3, 2, 1):
             wx_copy(j, k).start()
 
-    def start_wy(i, _):
-        wy_copy(i).start()
-        return 0
-
+    def wait_wx(j):
+        for k in (1, 2, 3):
+            wx_copy(j, k).wait_recv()
+
+    start_wx(0)
     wz.start()
-    start_wx(0)
+    start_wx(1)
 
     row_copy = remote(r_other, r_all.at[pl.ds(TOK, TOK)], row_s, row_r, sibling)
     pltpu.make_async_copy(r_other, r_other, local_sem.at[3]).wait()
@@ -323,9 +310,6 @@
             part = slice(s * 128, (s + 1) * 128)
             qr[:, :, s, :, lanes] = q_pad[:, :, :, part]
             cr[:, :, s, :, lanes] = c_pad[:, :, :, part]
-
-    wz.forward()
-    lax.fori_loop(1, 16, start_wy, 0)
 
     row_i = lax.broadcasted_iota(jnp.int32, (128, 256), 0)
     col_i = lax.broadcasted_iota(jnp.int32, (128, 256), 1)
@@ -380,14 +364,9 @@
     g_r[p] = g_s[p]
     pt_r[p] = pt_s[p]
 
-    def wait_wx(j):
-        for k in (1, 2, 3):
-            wx_copy(j, k).wait_recv()
-
-    wz.finish()
-    step_wz2(0)
     wait_wx(0)
     wx2[0].start()
+    wz.forward()
 
     pltpu.make_async_copy(r_other, r_other, local_sem.at[4]).wait()
 
@@ -410,6 +389,13 @@
 
     lax.fori_loop(1, 16, start_p, 0)
 
+    wz.finish()
+    wz2[0].step(0)
+    wait_wx(1)
+    wx2[1].start()
+    wz2[1].step(0)
+    wx2[0].forward()
+
     def wait_g(i, _):
         o = (p + i) % 16
         remote(g_s.at[o], g_r.at[o], g_ss.at[o], g_rs.at[o], (o, f)).wait_recv()
@@ -422,29 +408,23 @@
     go_copy = remote(g_own.at[pl.ds(0, TOK)], g_own.at[pl.ds(TOK, TOK)], go_s, go_r, sibling)
     go_copy.start()
 
-    wx2[0].forward()
-
-    def wait_wy(i, _):
-        wy_copy(i).wait_recv()
-        return 0
-
-    lax.fori_loop(1, 16, wait_wy, 0)
-    wy2.start()
-
     row_copy.wait()
     go_copy.wait()
 
     def a_part(q):
         def part(xx, half):
             return gt.at[
-                pl.ds(q * 128 + half * 64, 64), pl.ds(pl.multiple_of(xx * 1024, 128), 1024)
+                pl.ds(q * PART_A + half * (PART_A // 2), PART_A // 2),
+                pl.ds(pl.multiple_of(xx * 1024, 128), 1024),
             ]
 
         return part
 
     def b_part(q):
         def part(yy, half):
-            return gt.at[pl.ds(pl.multiple_of(256 + yy * 64 + q * 32 + half * 16, 16), 16)]
+            return gt.at[
+                pl.ds(pl.multiple_of(256 + yy * 64 + q * PART_B, 16), PART_B), pl.ds(half * 2048, 2048)
+            ]
 
         return part
 
@@ -459,6 +439,12 @@
     def partial(d):
         col = pl.ds(pl.multiple_of(((x + d) % 4) * 1024, 128), 1024)
         gt[:, col] = dot(gw[...], r_all[:, col]).astype(BF16)
+
+    def begin(q):
+        for i in range(4):
+            ring_a[q].copy(i).start()
+        for i in range(4):
+            ring_b[q].copy(i).start()
 
     partial(2)
     ring_a[0].copy(0).start()
@@ -470,27 +456,27 @@
     partial(0)
     for i in range(4):
         ring_b[0].copy(i).start()
-    for i in range(4):
-        ring_a[1].copy(i).start()
-    for i in range(4):
-        ring_b[1].copy(i).start()
-
-    step_wz2(1)
+    for q in range(1, PARTS):
+        begin(q)
+
+    wx2[1].forward()
+
+    wz2[0].step(1)
+    wz2[1].step(1)
 
     ring_a[0].forward()
-
     ring_b[0].forward()
 
-    step_wz2(2)
+    wz2[0].step(2)
 
     ring_a[1].forward()
-
     ring_b[1].forward()
 
-    wy2.forward()
+    wz2[0].step(3)
+    wz2[1].step(2)
 
     def a2_copy(q, d):
-        part = a1.at[q, pl.ds(pl.multiple_of(((y + d) % 4) * 32, 16), 32)]
+        part = a1.at[q, pl.ds(pl.multiple_of(((y + d) % 4) * PART_B, 16), PART_B)]
         i = q * 3 + d - 1
         return remote(part, a2_r.at[q, d - 1], a2_ss.at[i], a2_rs.at[i], at_y(d))
 
@@ -499,48 +485,31 @@
         i = q * 3 + d - 1
         return remote(part, b2_r.at[q, d - 1], b2_ss.at[i], b2_rs.at[i], at_x(d))
 
-    def second_a(q):
+    def second(q):
         ring_a[q].finish()
         for half in range(2):
-            a1[q, half * 64:(half + 1) * 64] = ring_a[q].total(half).astype(BF16)
+            rows = slice(half * (PART_A // 2), (half + 1) * (PART_A // 2))
+            a1[q, rows] = ring_a[q].total(half).astype(BF16)
         for d in (2, 1, 3):
             a2_copy(q, d).start()
-
-    def second_b(q):
         ring_b[q].finish()
         for half in range(2):
-            b1[q, half * 16:(half + 1) * 16] = ring_b[q].total(half).astype(BF16)
+            b1[q, :, half * 2048:(half + 1) * 2048] = ring_b[q].total(half).astype(BF16)
         for d in (2, 1, 3):
             b2_copy(q, d).start()
 
-    second_a(0)
-    second_b(0)
-
-    step_wz2(3)
-
-    second_a(1)
-
-    second_b(1)
-
-    for ring in wx2 + [wy2]:
-        ring.finish()
-    step_wz2(4)
-
-    for n in range(2):
-        cols = slice(n * 256, (n + 1) * 256)
-        v_s[:, cols] = dot(r_all[...], w_all[:, :, :, cols].reshape(DH, 256))
-    v_copy = remote(v_s.at[pl.ds(TOK, TOK)], v_r, v_ss, v_rs, sibling)
-    v_copy.start()
-
-    own_a = pl.ds(pl.multiple_of(y * 32, 16), 32)
+    second(0)
+
+    wz2[1].step(3)
+
+    second(1)
+
+    own_a = pl.ds(pl.multiple_of(y * PART_B, 16), PART_B)
     own_cols = pl.ds(pl.multiple_of(x * 1024, 128), 1024)
 
     def z_part(q, zz):
         zz = lax.rem(zz, 8)
-        return s3.at[
-            q, :, pl.ds(pl.multiple_of((zz % 2) * 16, 16), 16),
-            pl.ds(pl.multiple_of((zz // 2) * DC, 128), DC),
-        ]
+        return s3.at[q, :, :, pl.ds(pl.multiple_of(zz * 128, 128), 128)]
 
     def z_copy(q, k):
         i = q * 7 + k - 1
@@ -562,9 +531,52 @@
         for k in (4, 3, 5, 2, 6, 1, 7):
             z_copy(q, k).start()
 
-    third(0)
-
-    third(1)
+    for q in range(PARTS // 2):
+        third(q)
+
+    for ring in wx2:
+        ring.finish()
+    for ring in wz2:
+        ring.step(4)
+
+
+    for n in range(2):
+        cols = slice(n * 256, (n + 1) * 256)
+        v_s[:, cols] = dot(r_all[...], w_all[:, :, :, cols].reshape(DH, 256))
+    v_copy = remote(v_s.at[pl.ds(TOK, TOK)], v_r, v_ss, v_rs, sibling)
+    v_copy.start()
+
+    for q in range(PARTS // 2, PARTS):
+        third(q)
+
+    def f_copy(q, i):
+        j = q * 7 + i - 1
+        part = fin.at[q, c, p // 2]
+        to = (p + i) % 16 if q == PARTS - 1 else (p // 2 + i) % 8 * 2 + c
+        return remote(part, part, f_ss.at[j], f_rs.at[j], (to, f))
+
+    def f_peers(q):
+        return range(1, 16 if q == PARTS - 1 else 8)
+
+    def fs_copy(q):
+        part = fin.at[q, c]
+        return remote(part, part, fs_s.at[q], fs_r.at[q], sibling)
+
+    wide_gain = own_gain.astype(F32)
+    last_gain = jnp.where(zl == 0, wide_gain[:, :HALF], wide_gain[:, HALF:]).reshape(1, 1, HALF)
+
+    def last(q):
+        for k in range(1, 8):
+            z_copy(q, k).wait_recv()
+        total = z_part(q, z)[...].astype(F32)
+        for k in range(7):
+            total = total + r3[q, k].astype(F32)
+        fin[q, c, p // 2] = (total * last_gain).astype(BF16)
+        for i in f_peers(q):
+            f_copy(q, i).start()
+
+    for q in range(PARTS // 2):
+        last(q)
 
     v_copy.wait()
     values = ((v_s[0:TOK] + v_r[...]) * inverse).astype(BF16)
@@ -580,6 +592,9 @@
         return 0
 
     lax.fori_loop(1, 16, wait_p, 0)
+
+    for q in range(PARTS // 2, PARTS):
+        last(q)
 
     def attend(i, _):
         for t in range(4):
@@ -592,33 +607,6 @@
         return 0
 
     lax.fori_loop(0, N_DP // 4, attend, 0)
-
-    def f_copy(q, i):
-        j = q * 7 + i - 1
-        part = fin.at[q, c, p // 2]
-        return remote(part, part, f_ss.at[j], f_rs.at[j], ((p // 2 + i) % 8 * 2 + c, f))
-
-    def fs_copy(q):
-        part = fin.at[q, c]
-        return remote(part, part, fs_s.at[q], fs_r.at[q], sibling)
-
-    def last(q):
-        for k in range(1, 8):
-            z_copy(q, k).wait_recv()
-        total = z_part(q, z)[...].astype(F32)
-        for k in range(7):
-            total = total + r3[q, k].astype(F32)
-        fin[q, c, p // 2] = (total * own_gain.astype(F32).reshape(1, 1, DC)).astype(BF16)
-
-        def start_f(i, _):
-            f_copy(q, i).start()
-            return 0
-
-        lax.fori_loop(1, 8, start_f, 0)
-
-    last(0)
-
-    last(1)
 
     out_copies = []
     for g in range(KV_HEADS):
@@ -631,28 +619,32 @@
         )
         out_copies[-1].start()
 
-    for q in range(PARTS):
-        for i in range(1, 8):
+    for q in range(PARTS - 1):
+        for i in f_peers(q):
             f_copy(q, i).wait_recv()
         fs_copy(q).start()
-    for q in range(PARTS):
+    for i in f_peers(PARTS - 1):
+        f_copy(PARTS - 1, i).wait_recv()
+    for q in range(PARTS - 1):
         fs_copy(q).wait_recv()
 
     for core in range(2):
-        for portion in range(2):
-            pieces = []
-            for i in range(16):
-                yy, q, zz = (i // 2 % 4, i // 8, i % 2) if portion == 0 else (i // 4, i // 2 % 2, i % 2)
-                pieces.append(fin[q, core, zz * 4 + yy, portion].astype(F32))
-            tall = jnp.concatenate(pieces, axis=0)
-            grad_ref[core * DC:(core + 1) * DC, portion * 256:(portion + 1) * 256] = tall.T
+        for zz in range(2):
+            for portion in range(2):
+                pieces = []
+                for i in range(4 * PARTS):
+                    q, yy = (i // 4, i % 4) if portion == 0 else (i % PARTS, i // PARTS)
+                    pieces.append(fin[q, core, zz * 4 + yy, portion].astype(F32))
+                tall = jnp.concatenate(pieces, axis=0)
+                first = core * DC + zz * HALF
+                grad_ref[first:first + HALF, portion * 256:(portion + 1) * 256] = tall.T
 
     for cp in out_copies:
         cp.wait()
-    for ring in wx2 + [wy2, wz] + wz2 + ring_a + ring_b:
+    for ring in wx2 + [wz] + wz2 + ring_a + ring_b:
         ring.wait_send()
     for k in (1, 2, 3):
-        for j in range(CHUNKS):
+        for j in range(len(CHUNKS)):
             wx_copy(j, k).wait_send()
         for q in range(PARTS):
             a2_copy(q, k).wait_send()
@@ -660,17 +652,38 @@
     for k in range(1, 8):
         for q in range(PARTS):
             z_copy(q, k).wait_send()
-            f_copy(q, k).wait_send()
     for q in range(PARTS):
+        for i in f_peers(q):
+            f_copy(q, i).wait_send()
+    for q in range(PARTS - 1):
         fs_copy(q).wait_send()
 
     def wait_sends(i, _):
-        wy_copy(i).wait_send()
         g_copy((p + i) % 16).wait_send()
         p_copy((p + i) % 16).wait_send()
         return 0
 
     lax.fori_loop(1, 16, wait_sends, 0)
+
+
+def results(returned_ref, gradient_ref, out_ref, grad_ref, out_buf, grad_buf, in_sem, out_sem):
+    arrive, leave = [], []
+    for i in range(6):
+        if i < 4:
+            rows = pl.ds(i * (TOK // 4), TOK // 4)
+            refs = returned_ref.at[rows], out_buf.at[rows], out_ref.at[rows]
+        else:
+            rows = pl.ds((i - 4) * (DSH // 2), DSH // 2)
+            refs = gradient_ref.at[rows], grad_buf.at[rows], grad_ref.at[rows]
+        arrive.append(pltpu.make_async_copy(refs[0], refs[1], in_sem.at[i]))
+        leave.append(pltpu.make_async_copy(refs[1], refs[2], out_sem.at[i]))
+    for cp in arrive:
+        cp.start()
+    for first, second in zip(arrive, leave):
+        first.wait()
+        second.start()
+    for cp in leave:
+        cp.wait()
 
 
 def on_device(rows_owned, target, offset, queries, keys, cotangent, segment, norm_gain, value_weight):
@@ -692,17 +705,17 @@
         vmem((N_DP, CAP, KVW), BF16),
         vmem((2 * TOK, KVW), BF16),
         vmem((KVW, DH), BF16),
-        vmem((PARTS, 2, 64, 1024), BF16),
-        vmem((PARTS, 2, 2, 64, 1024), BF16),
-        vmem((PARTS, 2, 16, DH), BF16),
-        vmem((PARTS, 2, 2, 16, DH), BF16),
-        vmem((PARTS, 3, 32, 1024), BF16),
-        vmem((PARTS, 3, 32, 1024), BF16),
-        vmem((PARTS, 128, 1024), BF16),
-        vmem((PARTS, 32, DH), BF16),
-        vmem((PARTS, 2, 32, 1024), BF16),
-        vmem((PARTS, 7, 2, 16, DC), BF16),
-        vmem((PARTS, 2, 8, 2, 16, DC), BF16),
+        vmem((PARTS, 2, PART_A // 2, 1024), BF16),
+        vmem((PARTS, 2, 2, PART_A // 2, 1024), BF16),
+        vmem((PARTS, 2, PART_B, 2048), BF16),
+        vmem((PARTS, 2, 2, PART_B, 2048), BF16),
+        vmem((PARTS, 3, PART_B, 1024), BF16),
+        vmem((PARTS, 3, PART_B, 1024), BF16),
+        vmem((PARTS, PART_A, 1024), BF16),
+        vmem((PARTS, PART_B, DH), BF16),
+        vmem((PARTS, 2, PART_B, 1024), BF16),
+        vmem((PARTS, 7, 2, PART_B, HALF), BF16),
+        vmem((PARTS, 2, 8, 2, PART_B, HALF), BF16),
         vmem((2 * TOK, KVW), F32),
         vmem((TOK, KVW), F32),
         vmem((N_DP, 2, KV_HEADS, 16, KVW), BF16),
@@ -712,14 +725,14 @@
         vmem((KVW, 2 * TOK), BF16),
         dma((5,)),
         dma, dma,
-        dma((3 * CHUNKS,)), dma((3 * CHUNKS,)), dma((16,)), dma((16,)),
-        dma((6 * CHUNKS,)), dma((6 * CHUNKS,)), dma((6,)), dma((6,)),
-        dma((6,)), dma((6,)), dma((4 * CHUNKS_Z,)), dma((4 * CHUNKS_Z,)),
+        dma((3 * len(CHUNKS),)), dma((3 * len(CHUNKS),)),
+        dma((6 * len(CHUNKS),)), dma((6 * len(CHUNKS),)),
+        dma((6,)), dma((6,)), dma((4 * len(CHUNKS_Z),)), dma((4 * len(CHUNKS_Z),)),
         dma((16,)), dma((16,)), dma((16,)), dma((16,)),
         dma, dma, dma, dma,
+        dma((24,)), dma((24,)), dma((24,)), dma((24,)),
         dma((12,)), dma((12,)), dma((12,)), dma((12,)),
-        dma((6,)), dma((6,)), dma((6,)), dma((6,)),
-        dma((14,)), dma((14,)), dma((14,)), dma((14,)), dma((2,)), dma((2,)),
+        dma((28,)), dma((28,)), dma((36,)), dma((36,)), dma((3,)), dma((3,)),
         dma((KV_HEADS,)),
     ]
     anywhere = pl.BlockSpec(memory_space=pl.ANY)
@@ -748,6 +761,17 @@
         norm_gain,
         value_weight,
     )
+    returned, gradient = pl.pallas_call(
+        results,
+        out_shape=(
+            jax.ShapeDtypeStruct((TOK, QW), BF16),
+            jax.ShapeDtypeStruct((DSH, KVW), F32),
+        ),
+        in_specs=[anywhere, anywhere],
+        out_specs=(anywhere, anywhere),
+        scratch_shapes=[vmem((TOK, QW), BF16), vmem((DSH, KVW), F32), dma((6,)), dma((6,))],
+        name="results",
+    )(returned, gradient)
     return (returned.reshape(1, 1, TOK, QW), gradient)
 
 

time: 84.2 us -> 82 us (0.974)
  local copies, waits for them, and re-layouts: 4.19 us -> 0 us
  Pallas kernels: 79.3 us -> 81.3 us
    unnamed x4 -> x0, local copies, waits for them, and re-layouts: 4.19 us -> none
    pallas_call x0 -> x1, Pallas kernels: none -> 2.8 us  [on_device(): pl.pallas_call(results, out_shape=(jax.ShapeDtypeStruct((TOK, QW), BF16),...]
where the time goes in v4:
time: 82 us; the launch traced here: 81.9 us
  Pallas kernels  81.3 us (99%)
    pallas_call x1, Pallas kernels, on_device(): pl.pallas_call(kernel, out_shape=(jax.ShapeDtypeStruct((TOK, QW), BF16),...  78.5 us
    pallas_call x1, Pallas kernels, on_device(): pl.pallas_call(results, out_shape=(jax.ShapeDtypeStruct((TOK, QW), BF16),...  2.8 us

profile of v4, /device:TPU:1, one launch (start us, length us, event | category | flops | bytes accessed | tf_op | source)
XLA Modules:
  0.0 81.9 jit_solution(5483871910402441280)
XLA Ops:
  0.6 78.5 %value_path.1 = (bf16[256,4096]{1,0:T(8,128)(2,1)}, f32[512,512]{1,0:T(8,128)}) custom-call(bf16[256,8192]{1,0:T(8,128)(2,1)} %bitcast.7, s32[1,256]{1,0:T(1,128)} %bitcast.12, bf16[256,4096]{1,0:T(8,128)(2,1)} %bitcast.8, bf16[256,512]{1,0:T(8,128)(2,1)} %bitcast.11, bf16[256,4096]{1,0:T(8,128)(2,1)} %bitcast.9, s32[1,256]{1,0:T(1,128)} %bitcast.13, ...), custom_call_target="tpu_custom_call" | custom-call | flops 8000000000 | bytes 16777216 | tf_op jit(solution)/shard_map/value_path/pallas_call | solution.py:740
  79.1 2.8 %results.1 = (bf16[256,4096]{1,0:T(8,128)(2,1)}, f32[512,512]{1,0:T(8,128)}) custom-call(bf16[256,4096]{1,0:T(8,128)(2,1)} %get-tuple-element.6.returned_ref, f32[512,512]{1,0:T(8,128)} %get-tuple-element.7.gradient_ref), custom_call_target="tpu_custom_call" | custom-call | tf_op jit(solution)/shard_map/results/pallas_call | solution.py:764
